TPU v7x, 32 devices: a whole 2x2x4 slice. The times are simulated.
32 devices in a mesh: inp: 16 (over z, x, core), frq: 2 (over y).
Axes of the slice: x: 2, y: 2, z: 4, core: 2. Of those that a mesh axis runs over, the one named last changes fastest.
Arguments:
- voltages: bfloat16 [1024, 8, 2048], P('inp', 'frq'), may hold values from -6 to 6
- history: bfloat16 [1024, 3, 2048], P('inp'), may hold values from -6 to 6
- window: float32 [4, 2048], replicated, may hold values from -3 to 3
Outputs:
- visibilities: float32 [1024, 16, 2, 1024], P('frq', 'inp')
All inputs are finite; a program needn't handle non-finite values.
Results may differ from a plain program's by a relative error of at most 0.0003.
Values may be sent and summed in bfloat16 or wider, within the bound.
A program may use at most 64 MiB of HBM per device.

v0:
```python
import math

import jax
import jax.numpy as jnp
from jax import lax
from jax.sharding import PartitionSpec as P

SAMPLES = 2048
CH_DEV = 1


def shifted(block, axis, distance):
    devices = range(lax.axis_size(axis))
    route = [(i - distance, i) for i in devices if i - distance in devices]
    return lax.ppermute(block, axis, route)


def dft_table(channels, samples, first_bin):
    chan_bins = jnp.arange(channels, dtype=jnp.int32) + first_bin
    positions = jnp.arange(samples, dtype=jnp.int32)
    turns = chan_bins[:, None] * positions[None, :] % samples
    phases = turns.astype(jnp.float32) * (2.0 * math.pi / samples)
    scaling = 1.0 / math.sqrt(samples)
    return jnp.stack([jnp.cos(phases), -jnp.sin(phases)], axis=1) * scaling


def gram_rows(samples_in, first_row, row_count):
    chans = samples_in.shape[0]
    frames = samples_in.shape[1]
    inputs = samples_in.shape[3]
    left_rows = lax.dynamic_slice_in_dim(samples_in, first_row, row_count, 3)
    real_left = left_rows.reshape(chans, 2 * frames, row_count)
    imag_left = jnp.stack([left_rows[:, :, 1], -left_rows[:, :, 0]], axis=2).reshape(
        chans, 2 * frames, row_count
    )
    stacked = jnp.stack([real_left, imag_left], axis=1)
    all_cols = samples_in.reshape(chans, 2 * frames, inputs)
    return jnp.einsum("cjkr,cks->rcjs", stacked, all_cols, precision=lax.Precision.HIGHEST)


def body(voltages, history, window):
    taps_back = window.shape[0] - 1
    frames = voltages.shape[1]
    earlier = shifted(voltages[:, frames - taps_back :, :], "frq", 1)
    leading = jnp.where(lax.axis_index("frq") == 0, history, earlier)
    extended = jnp.concatenate([leading, voltages], axis=1).astype(jnp.float32)
    filtered = window[0] * extended[:, 0:frames, :]
    for tap_index in range(1, taps_back + 1):
        filtered = filtered + window[tap_index] * extended[:, tap_index : tap_index + frames, :]
    channels = CH_DEV * lax.axis_size("inp")
    first_bin = (SAMPLES // 2 - channels) // 2
    weights = dft_table(channels, SAMPLES, first_bin)
    spectra = jnp.einsum("cpn,itn->ctpi", weights, filtered, precision=lax.Precision.HIGHEST)
    turned = lax.all_to_all(spectra, "inp", split_axis=0, concat_axis=3, tiled=True)
    total_frames = frames * lax.axis_size("frq")
    tile_rows = turned.shape[3] // lax.axis_size("frq")
    anchor = lax.axis_index("frq") * tile_rows
    summed = gram_rows(lax.all_gather(turned, "frq", axis=1, tiled=True), anchor, tile_rows)
    return summed / total_frames


def solution(mesh):
    return jax.shard_map(
        body,
        mesh=mesh,
        in_specs=(P("inp", "frq", None), P("inp", None, None), P()),
        out_specs=P("frq", "inp", None, None),
        check_vma=False,
    )
```

profile of v0, /device:TPU:0, one launch (start us, length us, event | category | flops | bytes accessed | tf_op | source)
XLA Modules:
  0.0 64.2 jit_solution(9936382738219062990)
XLA Ops:
  0.0 0.0 copy-start.2
  0.0 0.0 copy-start.1
  0.0 1.9 %slice.34 = bf16[64,3,2048]{2,1,0:T(4,128)(2,1)S(1)} slice(bf16[64,4,2048]{2,1,0:T(4,128)(2,1)} %param.3), slice={[0:64], [1:4], [0:2048]} | slice | bytes 1572864 | tf_op jit(solution)/shard_map/slice | solution.py:44
  1.9 0.6 copy.23
  2.5 4.9 %collective-permute-start = (bf16[64,3,2048]{2,0,1:T(8,128)(2,1)S(1)}, bf16[64,3,2048]{2,0,1:T(8,128)(2,1)S(1)}, u32[]{:S(2)}, u32[]{:S(2)}) collective-permute-start(bf16[64,3,2048]{2,0,1:T(8,128)(2,1)S(1)} %copy.23), channel_id=1, source_target_pairs={{0,1},{2,3},{4,5},{6,7},{8,9},{10,11},{12,13},{14,15},{16,17},{18,... | collective-permute-start | bytes 2359304 | tf_op jit(solution)/shard_map/ppermute | solution.py:15
  7.5 0.0 copy-done.2
  7.5 0.6 fusion.22
  8.1 0.0 copy-start
  8.1 16.1 %collective-permute-done = bf16[64,3,2048]{2,0,1:T(8,128)(2,1)S(1)} collective-permute-done((bf16[64,3,2048]{2,0,1:T(8,128)(2,1)S(1)}, bf16[64,3,2048]{2,0,1:T(8,128)(2,1)S(1)}, u32[]{:S(2)}, u32[]{:S(2)}) %collective-permute-start) | collective-permute-done | bytes 786464 | tf_op jit(solution)/shard_map/ppermute | solution.py:15
  24.2 0.0 copy-done.1
  24.2 0.1 broadcast_select_fusion
  24.3 0.7 %copy.14 = bf16[64,3,2048]{2,1,0:T(4,128)(2,1)S(1)} copy(bf16[64,3,2048]{2,0,1:T(8,128)(2,1)S(1)} %broadcast_select_fusion) | data formatting | bytes 1572864 | tf_op jit(solution)/shard_map/jit(_where)/select_n | solution.py:45
  24.9 0.0 copy-done
  25.0 1.0 %maximum_convert_fusion = f32[64,7,2048]{2,1,0:T(8,128)S(1)} fusion(bf16[64,4,2048]{2,1,0:T(4,128)(2,1)S(1)} %copy-done, bf16[64,3,2048]{2,1,0:T(4,128)(2,1)S(1)} %copy.14), kind=kLoop, calls=%fused_computation.9 | loop fusion | flops 3670016 | bytes 5505024 | tf_op jit(solution)/shard_map/convert_element_type | solution.py:46
  26.0 1.8 %fusion.1 = f32[64,4,2048,1]{2,1,0,3:T(4,128)S(1)} fusion(f32[64,7,2048]{2,1,0:T(8,128)S(1)} %maximum_convert_fusion, f32[2048]{0:T(1024)S(1)} %bitcast.35, f32[2048]{0:T(1024)S(1)} %bitcast.36, f32[2048]{0:T(1024)S(1)} %bitcast.34, f32[2048]{0:T(1024)S(1)} %bitcast.33), kind=kLoop, calls=%fused_computation.3 | loop fusion | flops 3670016 | bytes 10518528 | tf_op jit(solution)/shard_map/add | solution.py:49
  27.8 3.9 %fusion.6 = f32[16,4,2,64]{3,0,2,1:T(8,128)S(1)} fusion(f32[64,4,2048,1]{2,1,0,3:T(4,128)S(1)} %fusion.1, f32[16,1,2048]{2,0,1:T(8,128)S(1)} %get-tuple-element.12, f32[16,1,2048]{2,0,1:T(8,128)S(1)} %get-tuple-element.11), kind=kOutput, calls=%fused_computation.12 | convolution fusion | flops 201457664 | bytes 2392064 | tf_op jit(solution)/shard_map/cpn,itn->ctpi/dot_general | solution.py:53
  31.8 0.7 %reshape.124 = f32[16,1,512]{2,1,0:T(1,128)} reshape(f32[16,4,2,64]{3,2,1,0:T(2,128)S(1)} %copy.16) | data formatting | bytes 65536
  32.5 5.9 %all-to-all-start = ((f32[16,1,512]{2,1,0:T(1,128)}), f32[16,1,512]{2,1,0:T(1,128)S(1)}, u32[]{:S(2)}, u32[]{:S(2)}) async-start(f32[16,1,512]{2,1,0:T(1,128)} %reshape.124), calls=%async_computation | async-start | bytes 65536 | tf_op jit(solution)/shard_map/all_to_all | solution.py:54
  38.4 6.6 %all-to-all-done = f32[16,1,512]{2,1,0:T(1,128)S(1)} async-done(((f32[16,1,512]{2,1,0:T(1,128)}), f32[16,1,512]{2,1,0:T(1,128)S(1)}, u32[]{:S(2)}, u32[]{:S(2)}) %all-to-all-start) | async-done | bytes 32800 | tf_op jit(solution)/shard_map/all_to_all | solution.py:54
  45.0 0.5 broadcast.123
  45.5 0.7 %reduce = f32[16,512]{1,0:T(8,128)S(1)} reduce(f32[16,1,512]{2,1,0:T(1,128)S(1)} %all-to-all-done, f32[]{:T(128)} %broadcast.123), dimensions={1}, to_apply=%all_to_all.13.reduce_sub_computation | reduce | bytes 65540 | tf_op jit(solution)/shard_map/all_to_all | solution.py:54
  46.3 0.1 reshape.125
  46.4 0.1 all_to_all.16
  46.5 5.0 %all_gather.3 = f32[1,8,2,1024]{3,2,0,1:T(2,128)S(1)} all-gather(f32[1,4,2,1024]{3,2,0,1:T(2,128)S(1)} %bitcast.32), channel_id=1, replica_groups=mesh['inp'=16,'frq'=2] {'frq'}, dimensions={1}, use_global_device_ids=true | all-gather | bytes 98304 | tf_op jit(solution)/shard_map/all_gather | solution.py:58
  51.6 0.1 constant_dynamic-slice_fusion
  51.8 5.1 %multiply_bitcast_fusion = f32[512,1,2,1024]{0,3,2,1:T(8,128)} fusion(f32[16,1024,1]{1,0,2:T(8,128)S(1)} %reshape.122, f32[1,1,16,512]{3,2,1,0:T(8,128)S(1)} %stack_reshape.7, f32[1,1,16,512]{3,2,1,0:T(8,128)S(1)} %stack_reshape.6), kind=kOutput, calls=%fused_computation | convolution fusion | flops 202391552 | bytes 4325376 | tf_op jit(solution)/shard_map/cjkr,cks->rcjs/dot_general | solution.py:38
  56.9 7.3 %copy.19 = f32[512,1,2,1024]{3,2,1,0:T(2,128)} copy(f32[512,1,2,1024]{0,3,2,1:T(8,128)} %multiply_bitcast_fusion) | data formatting | bytes 8388608 | tf_op jit(solution)/shard_map/div | solution.py:59
  (9 shorter events, 0.2 us)
Async XLA Ops:
  0.0 7.5 %copy-start.2 = (f32[4,2048]{1,0:T(4,128)S(1)}, f32[4,2048]{1,0:T(4,128)}, u32[]{:S(2)}) copy-start(f32[4,2048]{1,0:T(4,128)} %param.5) | copy-start | bytes 98308
  0.0 24.2 %copy-start.1 = (bf16[64,3,2048]{2,0,1:T(8,128)(2,1)S(1)}, bf16[64,3,2048]{2,0,1:T(8,128)(2,1)}, u32[]{:S(2)}) copy-start(bf16[64,3,2048]{2,0,1:T(8,128)(2,1)} %param.4) | copy-start | bytes 2359300
  2.5 21.7 %collective-permute-start = (bf16[64,3,2048]{2,0,1:T(8,128)(2,1)S(1)}, bf16[64,3,2048]{2,0,1:T(8,128)(2,1)S(1)}, u32[]{:S(2)}, u32[]{:S(2)}) collective-permute-start(bf16[64,3,2048]{2,0,1:T(8,128)(2,1)S(1)} %copy.23), channel_id=1, source_target_pairs={{0,1},{2,3},{4,5},{6,7},{8,9},{10,11},{12,13},{14,15},{16,17},{18,... | collective-permute-start | bytes 2359304 | tf_op jit(solution)/shard_map/ppermute | solution.py:15
  8.1 16.8 %copy-start = (bf16[64,4,2048]{2,1,0:T(4,128)(2,1)S(1)}, bf16[64,4,2048]{2,1,0:T(4,128)(2,1)}, u32[]{:S(2)}) copy-start(bf16[64,4,2048]{2,1,0:T(4,128)(2,1)} %param.3) | copy-start | bytes 3145732
  32.5 12.6 %all-to-all-start = ((f32[16,1,512]{2,1,0:T(1,128)}), f32[16,1,512]{2,1,0:T(1,128)S(1)}, u32[]{:S(2)}, u32[]{:S(2)}) async-start(f32[16,1,512]{2,1,0:T(1,128)} %reshape.124), calls=%async_computation | async-start | bytes 65536 | tf_op jit(solution)/shard_map/all_to_all | solution.py:54
where the time goes:
time: 64.6 us; the launch traced here: 64.2 us
  waiting for transfers between devices  22.7 us (35%)
  local copies, waits for them, and re-layouts  12.1 us (19%)
  starting transfers between devices  10.8 us (17%)
  matrix products  9.03 us (14%)
  blocking collectives  5.02 us (8%)
  other arithmetic  4.4 us (7%)
    ppermute x1, waiting for transfers between devices, shifted(): return lax.ppermute(block, axis, route)  16.1 us
    div x1, local copies, waits for them, and re-layouts, body(): return summed / total_frames  7.29 us
    all_to_all x1, waiting for transfers between devices, body(): lax.all_to_all(spectra, 'inp', split_axis=0, concat_axis=3, tiled=True)  6.63 us
    all_to_all x1, starting transfers between devices, body(): lax.all_to_all(spectra, 'inp', split_axis=0, concat_axis=3, tiled=True)  5.91 us
    dot_general x1, matrix products, gram_rows(): jnp.einsum('cjkr,cks->rcjs', stacked, all_cols, precision=lax.Precision.H...  5.15 us
    all_gather x1, blocking collectives, body(): lax.all_gather(turned, 'frq', axis=1, tiled=True)  5.02 us
    ppermute x1, starting transfers between devices, shifted(): return lax.ppermute(block, axis, route)  4.92 us
    dot_general x1, matrix products, body(): jnp.einsum('cpn,itn->ctpi', weights, filtered, precision=lax.Precision.HI...  3.88 us
  transfers between devices with their start and end apart: 2, of which 2 were waited for; matrix products, arithmetic and copies ran while one was open for 1% of the time, Pallas kernels for 0%

commit v1 on v0

v1 whole, which is shorter than its diff:
```python
import functools
import math

import jax
import jax.numpy as jnp
import numpy as np
from jax import lax
from jax.experimental import pallas as pl
from jax.experimental.pallas import tpu as pltpu
from jax.sharding import PartitionSpec as P

CH_DEV = 1
LANES = 128
SUBL = 8
MESH = pl.DeviceIdType.MESH


def dft_rows(channels, samples):
    first_bin = (samples // 2 - channels) // 2
    bins = np.arange(channels, dtype=np.int64) + first_bin
    turns = bins[:, None] * np.arange(samples, dtype=np.int64)[None, :] % samples
    phases = turns * (2.0 * math.pi / samples)
    table = np.concatenate([np.cos(phases), -np.sin(phases)], axis=0) / math.sqrt(samples)
    return table.astype(np.float32)


def split_bf16(value, pieces):
    out = []
    for _ in range(pieces):
        piece = value.astype(jnp.bfloat16)
        out.append(piece)
        value = value - piece.astype(jnp.float32)
    return out


def spectra_kernel(
    cfg, x_hbm, h_hbm, table_hbm, window_hbm, out_ref,
    x_scr, table_scr, window_scr, mat_scr, z_scr, msg_scr, recv_scr,
    in_sem, send_sem, recv_sem,
):
    n_inp, n_frq, n_loc, frames, hpad, taps, channels = cfg
    n_dev = n_inp * n_frq
    my_inp = lax.axis_index("inp")
    my_frq = lax.axis_index("frq")
    me = my_inp * n_frq + my_frq
    v_rows = n_loc * frames
    loads = [
        pltpu.make_async_copy(table_hbm, table_scr, in_sem.at[0]),
        pltpu.make_async_copy(window_hbm, window_scr, in_sem.at[1]),
        pltpu.make_async_copy(x_hbm, x_scr.at[pl.ds(0, v_rows)], in_sem.at[2]),
        pltpu.make_async_copy(h_hbm, x_scr.at[pl.ds(v_rows, n_loc * hpad)], in_sem.at[3]),
    ]
    for load in loads:
        load.start()

    barrier = pltpu.get_barrier_semaphore()

    def greet(step, carry):
        dest = lax.rem(me + step, n_dev)
        pl.semaphore_signal(
            barrier, inc=1, device_id=(dest // n_frq, dest % n_frq), device_id_type=MESH
        )
        return carry

    lax.fori_loop(1, n_dev, greet, 0)

    loads[0].wait()
    loads[1].wait()
    group = 2 * channels
    for tap in range(taps):
        hi, lo = split_bf16(window_scr[tap : tap + 1, :] * table_scr[...], 2)
        mat_scr[tap * group : (tap + 1) * group, :] = hi
        mat_scr[(taps + tap) * group : (taps + tap + 1) * group, :] = lo
    loads[2].wait()
    loads[3].wait()
    z = lax.dot_general(
        x_scr[...], mat_scr[...], (((1,), (1,)), ((), ())), preferred_element_type=jnp.float32
    )
    half = taps * group
    tiles = half // LANES
    for tile in range(tiles):
        z_scr[tile] = (
            z[:, tile * LANES : (tile + 1) * LANES]
            + z[:, half + tile * LANES : half + (tile + 1) * LANES]
        )

    first = my_frq == 0

    def frame(tile, u):
        if u >= frames:
            return None
        if u >= 0:
            return z_scr[tile, pl.ds(u, n_loc, stride=frames), :]
        rows = z_scr[tile, pl.ds(v_rows + u + taps - 1, n_loc, stride=hpad), :]
        return jnp.where(first, rows, 0.0)

    held = {(tile, u): frame(tile, u) for tile in range(tiles) for u in range(1 - taps, frames)}
    per_tile = LANES // group
    lane_group = lax.broadcasted_iota(jnp.int32, (n_loc, LANES), 1) // group
    per_lane = LANES // n_loc
    n_q = 2 * frames // per_lane
    msg_rows = msg_scr.shape[0] // channels

    def frame_products(tile, t):
        total = jnp.zeros((n_loc, LANES), jnp.float32)
        for g in range(per_tile):
            u = t - (taps - 1) + tile * per_tile + g
            part = held.get((tile, u))
            if part is not None:
                total = jnp.where(lane_group == g, part, total)
        return total

    for q in range(n_q):
        acc = None
        for tile in range(tiles):
            block = jnp.concatenate(
                [frame_products(tile, q * per_lane + c) for c in range(per_lane)], axis=0
            ).T
            for g in range(per_tile):
                part = block[g * group : (g + 1) * group]
                acc = part if acc is None else acc + part
        for part in range(2):
            for jb in range(channels // SUBL):
                row = part * channels + jb * SUBL
                msg_scr[
                    pl.ds(jb * SUBL * msg_rows + part * n_q + q, SUBL, stride=msg_rows), :
                ] = acc[row : row + SUBL]
    if msg_rows > 2 * n_q:
        for row in range(2 * n_q, msg_rows):
            for jb in range(channels // SUBL):
                msg_scr[pl.ds(jb * SUBL * msg_rows + row, SUBL, stride=msg_rows), :] = jnp.zeros(
                    (SUBL, LANES), jnp.float32
                )

    recv_scr[pl.ds(pl.multiple_of(me * msg_rows, SUBL), msg_rows), :] = msg_scr[
        pl.ds(pl.multiple_of(my_inp * msg_rows, SUBL), msg_rows), :
    ]
    pl.semaphore_wait(barrier, n_dev - 1)

    def send(step, carry):
        dest = lax.rem(me + step, n_dev)
        to_inp = dest // n_frq
        pltpu.make_async_remote_copy(
            src_ref=msg_scr.at[pl.ds(pl.multiple_of(to_inp * msg_rows, SUBL), msg_rows)],
            dst_ref=recv_scr.at[pl.ds(pl.multiple_of(me * msg_rows, SUBL), msg_rows)],
            send_sem=send_sem,
            recv_sem=recv_sem,
            device_id=(to_inp, dest % n_frq),
            device_id_type=MESH,
        ).start()
        return carry

    lax.fori_loop(1, n_dev, send, 0)
    everything = pltpu.make_async_remote_copy(
        src_ref=recv_scr.at[pl.ds(0, (n_dev - 1) * msg_rows)],
        dst_ref=recv_scr.at[pl.ds(0, (n_dev - 1) * msg_rows)],
        send_sem=send_sem,
        recv_sem=recv_sem,
        device_id=(my_inp, my_frq),
        device_id_type=MESH,
    )
    everything.wait_recv()

    row = lax.broadcasted_iota(jnp.int32, (msg_rows, LANES), 0)
    own = (row % n_q < n_q // 2) & (row < 2 * n_q)
    later = (row % n_q >= n_q // 2) & (row < 2 * n_q)
    lane_part = lax.broadcasted_iota(jnp.int32, (msg_rows, LANES), 1) // n_loc

    for m in range(n_inp // per_lane):
        msgs = [
            [
                recv_scr[((m * per_lane + e) * n_frq + f) * msg_rows :
                         ((m * per_lane + e) * n_frq + f + 1) * msg_rows, :]
                for e in range(per_lane)
            ]
            for f in range(n_frq)
        ]
        for c in range(per_lane):
            lined = []
            for f in range(n_frq):
                tile = None
                for e in range(per_lane):
                    turn = (e - c) * n_loc % LANES
                    piece = pltpu.roll(msgs[f][e], turn, 1) if turn else msgs[f][e]
                    tile = piece if tile is None else jnp.where(lane_part == e, piece, tile)
                lined.append(tile)
            shift = n_q // 2
            for pair in range(n_frq // 2):
                even, odd = lined[2 * pair], lined[2 * pair + 1]
                total = even + jnp.where(later, pltpu.roll(odd, shift, 0), 0.0)
                if pair:
                    before = pltpu.roll(lined[2 * pair - 1], msg_rows - shift, 0)
                    total = total + jnp.where(own, before, 0.0)
                at = (pair * per_lane + c) * msg_rows
                out_ref[at : at + msg_rows, m * LANES : (m + 1) * LANES] = total
    everything.wait_send()


def gram_kernel(cfg, spec_ref, out_ref, right_scr):
    n_q, msg_rows, row_block, total_frames, rows_dev = cfg
    depth, inputs = spec_ref.shape
    step = pl.program_id(0)

    @pl.when(step == 0)
    def _():
        h, m, l = split_bf16(spec_ref[...], 3)
        right_scr[...] = jnp.concatenate([h, m, h, l, h, m], axis=0)

    start = pl.multiple_of(lax.axis_index("frq") * rows_dev + step * row_block, LANES)
    left = spec_ref[:, pl.ds(start, row_block)] * (1.0 / total_frames)
    row = lax.broadcasted_iota(jnp.int32, left.shape, 0) % msg_rows
    swapped = jnp.concatenate(
        [
            jnp.where(
                row[:msg_rows] < n_q,
                pltpu.roll(left[at : at + msg_rows], msg_rows - n_q, 0),
                -pltpu.roll(left[at : at + msg_rows], n_q, 0),
            )
            for at in range(0, depth, msg_rows)
        ],
        axis=0,
    )
    h, m, l = split_bf16(jnp.concatenate([left, swapped], axis=1), 3)
    stack = jnp.concatenate([h, h, m, h, l, m], axis=0)
    vis = lax.dot_general(
        stack, right_scr[...], (((0,), (0,)), ((), ())), preferred_element_type=jnp.float32
    )
    per_row = 2 * inputs // LANES
    for part in range(2):
        for rb in range(row_block // SUBL):
            at = part * row_block + rb * SUBL
            for tile in range(inputs // LANES):
                out_ref[pl.ds(rb * SUBL * per_row + 2 * tile + part, SUBL, stride=per_row), :] = vis[
                    at : at + SUBL, tile * LANES : (tile + 1) * LANES
                ]


def body(n_inp, n_frq, voltages, history, window):
    n_loc, frames, samples = voltages.shape
    taps = window.shape[0]
    inputs = n_loc * n_inp
    channels = CH_DEV * n_inp
    hpad = -(-(taps - 1) // 4) * 4
    x = voltages.reshape(n_loc * frames, samples)
    h = jnp.pad(history, ((0, 0), (0, hpad - (taps - 1)), (0, 0))).reshape(n_loc * hpad, samples)
    table = jnp.asarray(dft_rows(channels, samples))

    per_lane = LANES // n_loc
    n_q = 2 * frames // per_lane
    msg_rows = -(-2 * n_q // SUBL) * SUBL
    depth = (n_frq // 2) * per_lane * msg_rows
    x_rows = n_loc * (frames + hpad)
    n_dev = n_inp * n_frq
    half = taps * 2 * channels
    spectra = pl.pallas_call(
        functools.partial(
            spectra_kernel, (n_inp, n_frq, n_loc, frames, hpad, taps, channels)
        ),
        out_shape=jax.ShapeDtypeStruct((depth, inputs), jnp.float32),
        in_specs=[pl.BlockSpec(memory_space=pl.ANY)] * 4,
        out_specs=pl.BlockSpec(memory_space=pltpu.VMEM),
        scratch_shapes=[
            pltpu.VMEM((x_rows, samples), jnp.bfloat16),
            pltpu.VMEM((2 * channels, samples), jnp.float32),
            pltpu.VMEM((taps, samples), jnp.float32),
            pltpu.VMEM((2 * half, samples), jnp.bfloat16),
            pltpu.VMEM((half // LANES, x_rows, LANES), jnp.float32),
            pltpu.VMEM((channels * msg_rows, LANES), jnp.float32),
            pltpu.VMEM((n_dev * msg_rows, LANES), jnp.float32),
            pltpu.SemaphoreType.DMA((4,)),
            pltpu.SemaphoreType.DMA,
            pltpu.SemaphoreType.DMA,
        ],
        compiler_params=pltpu.CompilerParams(
            collective_id=0, has_side_effects=True, vmem_limit_bytes=32 * 2**20
        ),
        name="spectra_exchange",
    )(x, h, table, window)

    rows_dev = inputs // n_frq
    row_block = min(LANES, rows_dev)
    per_row = 2 * inputs // LANES
    vis = pl.pallas_call(
        functools.partial(
            gram_kernel, (n_q, msg_rows, row_block, frames * n_frq, rows_dev)
        ),
        grid=(rows_dev // row_block,),
        out_shape=jax.ShapeDtypeStruct((rows_dev * per_row, LANES), jnp.float32),
        in_specs=[pl.BlockSpec((depth, inputs), lambda i: (0, 0))],
        out_specs=pl.BlockSpec((row_block * per_row, LANES), lambda i: (i, 0)),
        scratch_shapes=[pltpu.VMEM((6 * depth, inputs), jnp.bfloat16)],
        compiler_params=pltpu.CompilerParams(vmem_limit_bytes=32 * 2**20),
        name="gram",
    )(spectra)
    return (
        vis.reshape(rows_dev, inputs // LANES, 2, LANES)
        .transpose(0, 2, 1, 3)
        .reshape(rows_dev, 1, 2, inputs)
    )


def solution(mesh):
    return jax.shard_map(
        functools.partial(body, mesh.shape["inp"], mesh.shape["frq"]),
        mesh=mesh,
        in_specs=(P("inp", "frq", None), P("inp", None, None), P()),
        out_specs=P("frq", "inp", None, None),
        check_vma=False,
    )
```

time: 64.6 us -> 18.6 us (0.29)
  waiting for transfers between devices: 22.7 us -> 0 us
  Pallas kernels: 0 us -> 14.4 us
  starting transfers between devices: 10.8 us -> 0 us
  matrix products: 9.03 us -> 0 us
  local copies, waits for them, and re-layouts: 12.1 us -> 4.02 us
  blocking collectives: 5.02 us -> 0 us
  other arithmetic: 4.4 us -> 0 us
    ppermute x1 -> x0, waiting for transfers between devices: 16.1 us -> none  [shifted(): return lax.ppermute(block, axis, route)]
    pallas_call x0 -> x2, Pallas kernels: none -> 14.4 us  [the longest x1 10.8 us: body(): pl.pallas_call(functools.partial(spectra_kernel, (n_inp, n_frq, n_loc, fr...]
    dot_general x2 -> x0, matrix products: 9.03 us -> none  [the longest x1 5.15 us: gram_rows(): jnp.einsum('cjkr,cks->rcjs', stacked, all_cols, precision=lax.Precision.H...]
    div x1 -> x0, local copies, waits for them, and re-layouts: 7.29 us -> none  [body(): return summed / total_frames]
    all_to_all x1 -> x0, waiting for transfers between devices: 6.63 us -> none  [body(): lax.all_to_all(spectra, 'inp', split_axis=0, concat_axis=3, tiled=True)]
    all_to_all x1 -> x0, starting transfers between devices: 5.91 us -> none  [body(): lax.all_to_all(spectra, 'inp', split_axis=0, concat_axis=3, tiled=True)]
    all_gather x1 -> x0, blocking collectives: 5.02 us -> none  [body(): lax.all_gather(turned, 'frq', axis=1, tiled=True)]
    ppermute x1 -> x0, starting transfers between devices: 4.92 us -> none  [shifted(): return lax.ppermute(block, axis, route)]
  transfers between devices with their start and end apart: 2 -> 0, of which waited for: 2 -> 0; matrix products, arithmetic and copies ran while one was open for 1% -> 0% of each run, Pallas kernels for 0% -> 0%
where the time goes in v1:
time: 18.6 us; the launch traced here: 18.5 us
  Pallas kernels  14.4 us (77%)
  local copies, waits for them, and re-layouts  4.02 us (22%)
    pallas_call x1, Pallas kernels, body(): pl.pallas_call(functools.partial(spectra_kernel, (n_inp, n_frq, n_loc, fr...  10.8 us
    pallas_call x1, Pallas kernels, body(): pl.pallas_call(functools.partial(gram_kernel, (n_q, msg_rows, row_block,...  3.59 us
    unnamed x5, local copies, waits for them, and re-layouts  1.82 us
    reshape x1, local copies, waits for them, and re-layouts, body(): x = voltages.reshape(n_loc * frames, samples)  1.38 us
    pad x1, local copies, waits for them, and re-layouts, body(): jnp.pad(history, ((0, 0), (0, hpad - (taps - 1)), (0, 0)))  0.55 us

profile of v1, /device:TPU:0, one launch (start us, length us, event | category | flops | bytes accessed | tf_op | source)
XLA Modules:
  0.0 18.5 jit_solution(6496747819796710522)
XLA Ops:
  0.0 0.0 copy-start
  0.0 0.0 copy-start.1
  0.0 1.4 %reshape.12.x_hbm = bf16[256,2048]{1,0:T(8,128)(2,1)S(1)} reshape(bf16[64,4,2048]{2,1,0:T(4,128)(2,1)} %param.4) | data formatting | bytes 2097152 | tf_op jit(solution)/shard_map/reshape | solution.py:244
  1.4 1.8 %copy.7 = bf16[64,3,2048]{2,1,0:T(4,128)(2,1)S(1)} copy(bf16[64,3,2048]{2,0,1:T(8,128)(2,1)} %param.5) | data formatting | bytes 1572864
  3.2 0.5 %pad.4.clone = bf16[64,4,2048]{2,1,0:T(4,128)(2,1)S(1)} pad(bf16[64,3,2048]{2,1,0:T(4,128)(2,1)S(1)} %copy.7, bf16[]{:T(256)} %constant.4.clone.1), padding=0_0x0_1x0_0 | pad | bytes 1835010 | tf_op jit(solution)/shard_map/jit(_pad)/pad | solution.py:245
  3.8 0.3 %reshape.13.h_hbm = bf16[256,2048]{1,0:T(8,128)(2,1)S(1)} reshape(bf16[64,4,2048]{2,1,0:T(4,128)(2,1)S(1)} %pad.4.clone) | data formatting | bytes 2097152 | tf_op jit(solution)/shard_map/reshape | solution.py:245
  4.0 0.0 copy-done
  4.1 0.0 copy-done.1
  4.1 10.8 %spectra_exchange.1.spec_ref = f32[16,1024]{1,0:T(8,128)S(1)} custom-call(bf16[256,2048]{1,0:T(8,128)(2,1)S(1)} %reshape.12.x_hbm, bf16[256,2048]{1,0:T(8,128)(2,1)S(1)} %reshape.13.h_hbm, f32[32,2048]{1,0:T(8,128)S(1)} %copy-done, f32[4,2048]{1,0:T(4,128)S(1)} %copy-done.1), custom_call_target="tpu_custom_call" | custom-call | tf_op jit(solution)/shard_map/spectra_exchange/pallas_call | solution.py:255
  14.9 3.6 %gram.1 = f32[8192,128]{1,0:T(8,128)} custom-call(f32[16,1024]{1,0:T(8,128)S(1)} %spectra_exchange.1.spec_ref), custom_call_target="tpu_custom_call" | custom-call | tf_op jit(solution)/shard_map/gram/pallas_call | solution.py:283
Async XLA Ops:
  0.0 4.0 %copy-start = (f32[32,2048]{1,0:T(8,128)S(1)}, f32[32,2048]{1,0:T(8,128)}, u32[]{:S(2)}) copy-start(f32[32,2048]{1,0:T(8,128)} %constant.5.clone.table_hbm) | copy-start | bytes 786436
  0.0 4.1 %copy-start.1 = (f32[4,2048]{1,0:T(4,128)S(1)}, f32[4,2048]{1,0:T(4,128)}, u32[]{:S(2)}) copy-start(f32[4,2048]{1,0:T(4,128)} %window_hbm.1) | copy-start | bytes 98308

commit v2 on v1

--- a/solution.py
+++ b/solution.py
@@ -35,10 +35,10 @@
 
 def spectra_kernel(
     cfg, x_hbm, h_hbm, table_hbm, window_hbm, out_ref,
-    x_scr, table_scr, window_scr, mat_scr, z_scr, msg_scr, recv_scr,
+    x_scr, h_scr, table_scr, window_scr, mat_scr, z_scr, msg_scr, recv_scr,
     in_sem, send_sem, recv_sem,
 ):
-    n_inp, n_frq, n_loc, frames, hpad, taps, channels = cfg
+    n_inp, n_frq, n_loc, frames, taps, channels = cfg
     n_dev = n_inp * n_frq
     my_inp = lax.axis_index("inp")
     my_frq = lax.axis_index("frq")
@@ -47,8 +47,8 @@
     loads = [
         pltpu.make_async_copy(table_hbm, table_scr, in_sem.at[0]),
         pltpu.make_async_copy(window_hbm, window_scr, in_sem.at[1]),
-        pltpu.make_async_copy(x_hbm, x_scr.at[pl.ds(0, v_rows)], in_sem.at[2]),
-        pltpu.make_async_copy(h_hbm, x_scr.at[pl.ds(v_rows, n_loc * hpad)], in_sem.at[3]),
+        pltpu.make_async_copy(h_hbm, h_scr, in_sem.at[2]),
+        pltpu.make_async_copy(x_hbm, x_scr, in_sem.at[3]),
     ]
     for load in loads:
         load.start()
@@ -71,18 +71,23 @@
         hi, lo = split_bf16(window_scr[tap : tap + 1, :] * table_scr[...], 2)
         mat_scr[tap * group : (tap + 1) * group, :] = hi
         mat_scr[(taps + tap) * group : (taps + tap + 1) * group, :] = lo
-    loads[2].wait()
-    loads[3].wait()
-    z = lax.dot_general(
-        x_scr[...], mat_scr[...], (((1,), (1,)), ((), ())), preferred_element_type=jnp.float32
-    )
     half = taps * group
     tiles = half // LANES
-    for tile in range(tiles):
-        z_scr[tile] = (
-            z[:, tile * LANES : (tile + 1) * LANES]
-            + z[:, half + tile * LANES : half + (tile + 1) * LANES]
+
+    def transform(rows, at):
+        z = lax.dot_general(
+            rows, mat_scr[...], (((1,), (1,)), ((), ())), preferred_element_type=jnp.float32
         )
+        for tile in range(tiles):
+            z_scr[tile, at : at + rows.shape[0]] = (
+                z[:, tile * LANES : (tile + 1) * LANES]
+                + z[:, half + tile * LANES : half + (tile + 1) * LANES]
+            )
+
+    loads[2].wait()
+    transform(h_scr[...], v_rows)
+    loads[3].wait()
+    transform(x_scr[...].reshape(v_rows, x_scr.shape[2]), 0)
 
     first = my_frq == 0
 
@@ -91,7 +96,8 @@
             return None
         if u >= 0:
             return z_scr[tile, pl.ds(u, n_loc, stride=frames), :]
-        rows = z_scr[tile, pl.ds(v_rows + u + taps - 1, n_loc, stride=hpad), :]
+        at = v_rows + (u + taps - 1) * n_loc
+        rows = z_scr[tile, at : at + n_loc, :]
         return jnp.where(first, rows, 0.0)
 
     held = {(tile, u): frame(tile, u) for tile in range(tiles) for u in range(1 - taps, frames)}
@@ -240,27 +246,26 @@
     taps = window.shape[0]
     inputs = n_loc * n_inp
     channels = CH_DEV * n_inp
-    hpad = -(-(taps - 1) // 4) * 4
-    x = voltages.reshape(n_loc * frames, samples)
-    h = jnp.pad(history, ((0, 0), (0, hpad - (taps - 1)), (0, 0))).reshape(n_loc * hpad, samples)
+    h = history.transpose(1, 0, 2).reshape((taps - 1) * n_loc, samples)
     table = jnp.asarray(dft_rows(channels, samples))
 
     per_lane = LANES // n_loc
     n_q = 2 * frames // per_lane
     msg_rows = -(-2 * n_q // SUBL) * SUBL
     depth = (n_frq // 2) * per_lane * msg_rows
-    x_rows = n_loc * (frames + hpad)
+    x_rows = n_loc * (frames + taps - 1)
     n_dev = n_inp * n_frq
     half = taps * 2 * channels
     spectra = pl.pallas_call(
         functools.partial(
-            spectra_kernel, (n_inp, n_frq, n_loc, frames, hpad, taps, channels)
+            spectra_kernel, (n_inp, n_frq, n_loc, frames, taps, channels)
         ),
         out_shape=jax.ShapeDtypeStruct((depth, inputs), jnp.float32),
         in_specs=[pl.BlockSpec(memory_space=pl.ANY)] * 4,
         out_specs=pl.BlockSpec(memory_space=pltpu.VMEM),
         scratch_shapes=[
-            pltpu.VMEM((x_rows, samples), jnp.bfloat16),
+            pltpu.VMEM((n_loc, frames, samples), jnp.bfloat16),
+            pltpu.VMEM(((taps - 1) * n_loc, samples), jnp.bfloat16),
             pltpu.VMEM((2 * channels, samples), jnp.float32),
             pltpu.VMEM((taps, samples), jnp.float32),
             pltpu.VMEM((2 * half, samples), jnp.bfloat16),
@@ -272,10 +277,10 @@
             pltpu.SemaphoreType.DMA,
         ],
         compiler_params=pltpu.CompilerParams(
-            collective_id=0, has_side_effects=True, vmem_limit_bytes=32 * 2**20
+            collective_id=0, has_side_effects=True, vmem_limit_bytes=60 * 2**20
         ),
         name="spectra_exchange",
-    )(x, h, table, window)
+    )(voltages, h, table, window)
 
     rows_dev = inputs // n_frq
     row_block = min(LANES, rows_dev)

time: 18.6 us -> 16.8 us (0.903)
  local copies, waits for them, and re-layouts: 4.02 us -> 0.83 us
  Pallas kernels: 14.4 us -> 15.7 us
    reshape x2 -> x0, local copies, waits for them, and re-layouts: 1.65 us -> none  [the longest x1 1.38 us: body(): x = voltages.reshape(n_loc * frames, samples)]
    pallas_call x1, Pallas kernels: 10.8 us -> 12.2 us  [body(): pl.pallas_call(functools.partial(spectra_kernel, (n_inp, n_frq, n_loc, fr...]
    unnamed x5 -> x2, local copies, waits for them, and re-layouts: 1.82 us -> 0.83 us
    pad x1 -> x0, local copies, waits for them, and re-layouts: 0.55 us -> none  [body(): jnp.pad(history, ((0, 0), (0, hpad - (taps - 1)), (0, 0)))]
where the time goes in v2:
time: 16.8 us; the launch traced here: 16.6 us
  Pallas kernels  15.7 us (93%)
  local copies, waits for them, and re-layouts  0.83 us (5%)
    pallas_call x1, Pallas kernels, body(): pl.pallas_call(functools.partial(spectra_kernel, (n_inp, n_frq, n_loc, fr...  12.2 us
    pallas_call x1, Pallas kernels, body(): pl.pallas_call(functools.partial(gram_kernel, (n_q, msg_rows, row_block,...  3.57 us
    unnamed x2, local copies, waits for them, and re-layouts  0.83 us

profile of v2, /device:TPU:0, one launch (start us, length us, event | category | flops | bytes accessed | tf_op | source)
XLA Modules:
  0.0 16.6 jit_solution(13994220961887481873)
XLA Ops:
  0.0 12.2 %spectra_exchange.1.spec_ref = f32[16,1024]{1,0:T(8,128)} custom-call(bf16[64,4,2048]{2,1,0:T(4,128)(2,1)} %x_hbm.1, bf16[192,2048]{1,0:T(8,128)(2,1)} %bitcast.8, f32[32,2048]{1,0:T(8,128)} %constant.2.clone.table_hbm, f32[4,2048]{1,0:T(4,128)} %window_hbm.1), custom_call_target="tpu_custom_call" | custom-call | tf_op jit(solution)/shard_map/spectra_exchange/pallas_call | solution.py:259
  12.2 0.0 copy-start
  12.2 0.8 %copy-done = f32[16,1024]{1,0:T(8,128)S(1)} copy-done((f32[16,1024]{1,0:T(8,128)S(1)}, f32[16,1024]{1,0:T(8,128)}, u32[]{:S(2)}) %copy-start) | copy-done | bytes 65560
  13.0 3.6 %gram.1 = f32[8192,128]{1,0:T(8,128)} custom-call(f32[16,1024]{1,0:T(8,128)S(1)} %copy-done), custom_call_target="tpu_custom_call" | custom-call | tf_op jit(solution)/shard_map/gram/pallas_call | solution.py:288
Async XLA Ops:
  12.2 0.8 %copy-start = (f32[16,1024]{1,0:T(8,128)S(1)}, f32[16,1024]{1,0:T(8,128)}, u32[]{:S(2)}) copy-start(f32[16,1024]{1,0:T(8,128)} %spectra_exchange.1.spec_ref) | copy-start | bytes 196612

commit v3 on v2

--- a/solution.py
+++ b/solution.py
@@ -34,8 +34,8 @@
 
 
 def spectra_kernel(
-    cfg, x_hbm, h_hbm, table_hbm, window_hbm, out_ref,
-    x_scr, h_scr, table_scr, window_scr, mat_scr, z_scr, msg_scr, recv_scr,
+    cfg, x_hbm, h_hbm, table_hbm, window_hbm, out_hbm,
+    x_scr, h_scr, table_scr, window_scr, mat_scr, z_scr, msg_scr,
     in_sem, send_sem, recv_sem,
 ):
     n_inp, n_frq, n_loc, frames, taps, channels = cfg
@@ -138,9 +138,13 @@
                     (SUBL, LANES), jnp.float32
                 )
 
-    recv_scr[pl.ds(pl.multiple_of(me * msg_rows, SUBL), msg_rows), :] = msg_scr[
-        pl.ds(pl.multiple_of(my_inp * msg_rows, SUBL), msg_rows), :
-    ]
+    my_slot = out_hbm.at[pl.ds(pl.multiple_of(me * msg_rows, SUBL), msg_rows)]
+    mine = pltpu.make_async_copy(
+        msg_scr.at[pl.ds(pl.multiple_of(my_inp * msg_rows, SUBL), msg_rows)],
+        my_slot,
+        in_sem.at[4],
+    )
+    mine.start()
     pl.semaphore_wait(barrier, n_dev - 1)
 
     def send(step, carry):
@@ -148,7 +152,7 @@
         to_inp = dest // n_frq
         pltpu.make_async_remote_copy(
             src_ref=msg_scr.at[pl.ds(pl.multiple_of(to_inp * msg_rows, SUBL), msg_rows)],
-            dst_ref=recv_scr.at[pl.ds(pl.multiple_of(me * msg_rows, SUBL), msg_rows)],
+            dst_ref=my_slot,
             send_sem=send_sem,
             recv_sem=recv_sem,
             device_id=(to_inp, dest % n_frq),
@@ -158,8 +162,8 @@
 
     lax.fori_loop(1, n_dev, send, 0)
     everything = pltpu.make_async_remote_copy(
-        src_ref=recv_scr.at[pl.ds(0, (n_dev - 1) * msg_rows)],
-        dst_ref=recv_scr.at[pl.ds(0, (n_dev - 1) * msg_rows)],
+        src_ref=out_hbm.at[pl.ds(0, (n_dev - 1) * msg_rows)],
+        dst_ref=out_hbm.at[pl.ds(0, (n_dev - 1) * msg_rows)],
         send_sem=send_sem,
         recv_sem=recv_sem,
         device_id=(my_inp, my_frq),
@@ -167,6 +171,18 @@
     )
     everything.wait_recv()
 
+    mine.wait()
+    everything.wait_send()
+
+
+def gram_kernel(cfg, msg_hbm, out_hbm, msg_scr, spec_ref, vis_scr, in_sem, out_sem):
+    n_inp, n_frq, n_loc, n_q, msg_rows, row_block, total_frames, rows_dev = cfg
+    depth, inputs = spec_ref.shape
+    per_lane = LANES // n_loc
+    load = pltpu.make_async_copy(msg_hbm, msg_scr, in_sem)
+    load.start()
+    load.wait()
+
     row = lax.broadcasted_iota(jnp.int32, (msg_rows, LANES), 0)
     own = (row % n_q < n_q // 2) & (row < 2 * n_q)
     later = (row % n_q >= n_q // 2) & (row < 2 * n_q)
@@ -175,7 +191,7 @@
     for m in range(n_inp // per_lane):
         msgs = [
             [
-                recv_scr[((m * per_lane + e) * n_frq + f) * msg_rows :
+                msg_scr[((m * per_lane + e) * n_frq + f) * msg_rows :
                          ((m * per_lane + e) * n_frq + f + 1) * msg_rows, :]
                 for e in range(per_lane)
             ]
@@ -198,47 +214,44 @@
                     before = pltpu.roll(lined[2 * pair - 1], msg_rows - shift, 0)
                     total = total + jnp.where(own, before, 0.0)
                 at = (pair * per_lane + c) * msg_rows
-                out_ref[at : at + msg_rows, m * LANES : (m + 1) * LANES] = total
-    everything.wait_send()
-
-
-def gram_kernel(cfg, spec_ref, out_ref, right_scr):
-    n_q, msg_rows, row_block, total_frames, rows_dev = cfg
-    depth, inputs = spec_ref.shape
-    step = pl.program_id(0)
-
-    @pl.when(step == 0)
-    def _():
-        h, m, l = split_bf16(spec_ref[...], 3)
-        right_scr[...] = jnp.concatenate([h, m, h, l, h, m], axis=0)
-
-    start = pl.multiple_of(lax.axis_index("frq") * rows_dev + step * row_block, LANES)
-    left = spec_ref[:, pl.ds(start, row_block)] * (1.0 / total_frames)
-    row = lax.broadcasted_iota(jnp.int32, left.shape, 0) % msg_rows
-    swapped = jnp.concatenate(
-        [
-            jnp.where(
-                row[:msg_rows] < n_q,
-                pltpu.roll(left[at : at + msg_rows], msg_rows - n_q, 0),
-                -pltpu.roll(left[at : at + msg_rows], n_q, 0),
+                spec_ref[at : at + msg_rows, m * LANES : (m + 1) * LANES] = total
+
+    h, m, l = split_bf16(spec_ref[...], 3)
+    right = jnp.concatenate([h, m, h, l, h, m], axis=0)
+    anchor = lax.axis_index("frq") * rows_dev
+    copies = []
+    for step in range(rows_dev // row_block):
+        start = pl.multiple_of(anchor + step * row_block, LANES)
+        left = spec_ref[:, pl.ds(start, row_block)] * (1.0 / total_frames)
+        row = lax.broadcasted_iota(jnp.int32, left.shape, 0) % msg_rows
+        swapped = jnp.concatenate(
+            [
+                jnp.where(
+                    row[:msg_rows] < n_q,
+                    pltpu.roll(left[at : at + msg_rows], msg_rows - n_q, 0),
+                    -pltpu.roll(left[at : at + msg_rows], n_q, 0),
+                )
+                for at in range(0, depth, msg_rows)
+            ],
+            axis=0,
+        )
+        for part, side in enumerate((left, swapped)):
+            h, m, l = split_bf16(side, 3)
+            stack = jnp.concatenate([h, h, m, h, l, m], axis=0)
+            vis = lax.dot_general(
+                stack, right, (((0,), (0,)), ((), ())), preferred_element_type=jnp.float32
             )
-            for at in range(0, depth, msg_rows)
-        ],
-        axis=0,
-    )
-    h, m, l = split_bf16(jnp.concatenate([left, swapped], axis=1), 3)
-    stack = jnp.concatenate([h, h, m, h, l, m], axis=0)
-    vis = lax.dot_general(
-        stack, right_scr[...], (((0,), (0,)), ((), ())), preferred_element_type=jnp.float32
-    )
-    per_row = 2 * inputs // LANES
-    for part in range(2):
-        for rb in range(row_block // SUBL):
-            at = part * row_block + rb * SUBL
+            rows = pl.ds(step * row_block, row_block)
             for tile in range(inputs // LANES):
-                out_ref[pl.ds(rb * SUBL * per_row + 2 * tile + part, SUBL, stride=per_row), :] = vis[
-                    at : at + SUBL, tile * LANES : (tile + 1) * LANES
-                ]
+                at = 2 * tile + part
+                vis_scr[at, rows, :] = vis[:, tile * LANES : (tile + 1) * LANES]
+                copy = pltpu.make_async_copy(
+                    vis_scr.at[at, rows], out_hbm.at[rows, at], out_sem.at[len(copies)]
+                )
+                copy.start()
+                copies.append(copy)
+    for copy in copies:
+        copy.wait()
 
 
 def body(n_inp, n_frq, voltages, history, window):
@@ -260,9 +273,9 @@
         functools.partial(
             spectra_kernel, (n_inp, n_frq, n_loc, frames, taps, channels)
         ),
-        out_shape=jax.ShapeDtypeStruct((depth, inputs), jnp.float32),
+        out_shape=jax.ShapeDtypeStruct((n_dev * msg_rows, LANES), jnp.float32),
         in_specs=[pl.BlockSpec(memory_space=pl.ANY)] * 4,
-        out_specs=pl.BlockSpec(memory_space=pltpu.VMEM),
+        out_specs=pl.BlockSpec(memory_space=pl.ANY),
         scratch_shapes=[
             pltpu.VMEM((n_loc, frames, samples), jnp.bfloat16),
             pltpu.VMEM(((taps - 1) * n_loc, samples), jnp.bfloat16),
@@ -271,8 +284,7 @@
             pltpu.VMEM((2 * half, samples), jnp.bfloat16),
             pltpu.VMEM((half // LANES, x_rows, LANES), jnp.float32),
             pltpu.VMEM((channels * msg_rows, LANES), jnp.float32),
-            pltpu.VMEM((n_dev * msg_rows, LANES), jnp.float32),
-            pltpu.SemaphoreType.DMA((4,)),
+            pltpu.SemaphoreType.DMA((5,)),
             pltpu.SemaphoreType.DMA,
             pltpu.SemaphoreType.DMA,
         ],
@@ -287,14 +299,20 @@
     per_row = 2 * inputs // LANES
     vis = pl.pallas_call(
         functools.partial(
-            gram_kernel, (n_q, msg_rows, row_block, frames * n_frq, rows_dev)
+            gram_kernel,
+            (n_inp, n_frq, n_loc, n_q, msg_rows, row_block, frames * n_frq, rows_dev),
         ),
-        grid=(rows_dev // row_block,),
-        out_shape=jax.ShapeDtypeStruct((rows_dev * per_row, LANES), jnp.float32),
-        in_specs=[pl.BlockSpec((depth, inputs), lambda i: (0, 0))],
-        out_specs=pl.BlockSpec((row_block * per_row, LANES), lambda i: (i, 0)),
-        scratch_shapes=[pltpu.VMEM((6 * depth, inputs), jnp.bfloat16)],
-        compiler_params=pltpu.CompilerParams(vmem_limit_bytes=32 * 2**20),
+        out_shape=jax.ShapeDtypeStruct((rows_dev, per_row, LANES), jnp.float32),
+        in_specs=[pl.BlockSpec(memory_space=pl.ANY)],
+        out_specs=pl.BlockSpec(memory_space=pl.ANY),
+        scratch_shapes=[
+            pltpu.VMEM((n_dev * msg_rows, LANES), jnp.float32),
+            pltpu.VMEM((depth, inputs), jnp.float32),
+            pltpu.VMEM((per_row, rows_dev, LANES), jnp.float32),
+            pltpu.SemaphoreType.DMA,
+            pltpu.SemaphoreType.DMA((rows_dev // row_block * per_row,)),
+        ],
+        compiler_params=pltpu.CompilerParams(vmem_limit_bytes=60 * 2**20),
         name="gram",
     )(spectra)
     return (

time: 16.8 us -> 15.5 us (0.923)
  local copies, waits for them, and re-layouts: 0.83 us -> 0 us
  Pallas kernels: 15.7 us -> 15.3 us
    unnamed x2 -> x0, local copies, waits for them, and re-layouts: 0.83 us -> none
    pallas_call x1, Pallas kernels: 12.2 us -> 11.6 us  [body(): pl.pallas_call(functools.partial(spectra_kernel, (n_inp, n_frq, n_loc, fr...]
    pallas_call x1, Pallas kernels: 3.57 us -> 3.74 us  [body(): pl.pallas_call(functools.partial(gram_kernel, (n_inp, n_frq, n_loc, n_q,...]
where the time goes in v3:
time: 15.5 us; the launch traced here: 15.3 us
  Pallas kernels  15.3 us (99%)
    pallas_call x1, Pallas kernels, body(): pl.pallas_call(functools.partial(spectra_kernel, (n_inp, n_frq, n_loc, fr...  11.6 us
    pallas_call x1, Pallas kernels, body(): pl.pallas_call(functools.partial(gram_kernel, (n_inp, n_frq, n_loc, n_q,...  3.74 us

profile of v3, /device:TPU:0, one launch (start us, length us, event | category | flops | bytes accessed | tf_op | source)
XLA Modules:
  0.0 15.3 jit_solution(7233730197644538532)
XLA Ops:
  0.0 11.6 %spectra_exchange.1.msg_hbm = f32[256,128]{1,0:T(8,128)} custom-call(bf16[64,4,2048]{2,1,0:T(4,128)(2,1)} %x_hbm.1, bf16[192,2048]{1,0:T(8,128)(2,1)} %bitcast.8, f32[32,2048]{1,0:T(8,128)} %constant.2.clone.table_hbm, f32[4,2048]{1,0:T(4,128)} %window_hbm.1), custom_call_target="tpu_custom_call" | custom-call | tf_op jit(solution)/shard_map/spectra_exchange/pallas_call | solution.py:272
  11.6 3.7 %gram.1 = f32[512,16,128]{2,1,0:T(8,128)} custom-call(f32[256,128]{1,0:T(8,128)} %spectra_exchange.1.msg_hbm), custom_call_target="tpu_custom_call" | custom-call | tf_op jit(solution)/shard_map/gram/pallas_call | solution.py:300

commit v4 on v3

--- a/solution.py
+++ b/solution.py
@@ -31,6 +31,20 @@
         out.append(piece)
         value = value - piece.astype(jnp.float32)
     return out
+
+
+def to_others(n_inp, n_frq, my_inp, my_frq, act):
+    def group(ahead, low):
+        to_inp = lax.rem(my_inp + ahead, n_inp)
+        for turn in range(low, n_frq):
+            act(to_inp, lax.rem(my_frq + turn, n_frq))
+
+    if n_inp * n_frq <= 32:
+        for step in range(n_inp - 1):
+            group((n_inp // 2 + step) % n_inp if step < n_inp // 2 else n_inp - 1 - step, 0)
+    else:
+        lax.fori_loop(1, n_inp, lambda step, carry: (group(step, 0), carry)[1], 0)
+    group(0, 1)
 
 
 def spectra_kernel(
@@ -55,14 +69,10 @@
 
     barrier = pltpu.get_barrier_semaphore()
 
-    def greet(step, carry):
-        dest = lax.rem(me + step, n_dev)
-        pl.semaphore_signal(
-            barrier, inc=1, device_id=(dest // n_frq, dest % n_frq), device_id_type=MESH
-        )
-        return carry
-
-    lax.fori_loop(1, n_dev, greet, 0)
+    def greet(to_inp, to_frq):
+        pl.semaphore_signal(barrier, inc=1, device_id=(to_inp, to_frq), device_id_type=MESH)
+
+    to_others(n_inp, n_frq, my_inp, my_frq, greet)
 
     loads[0].wait()
     loads[1].wait()
@@ -74,20 +84,17 @@
     half = taps * group
     tiles = half // LANES
 
-    def transform(rows, at):
-        z = lax.dot_general(
-            rows, mat_scr[...], (((1,), (1,)), ((), ())), preferred_element_type=jnp.float32
+    loads[2].wait()
+    loads[3].wait()
+    rows = jnp.concatenate([x_scr[...].reshape(v_rows, x_scr.shape[2]), h_scr[...]], axis=0)
+    z = lax.dot_general(
+        rows, mat_scr[...], (((1,), (1,)), ((), ())), preferred_element_type=jnp.float32
+    )
+    for tile in range(tiles):
+        z_scr[tile] = (
+            z[:, tile * LANES : (tile + 1) * LANES]
+            + z[:, half + tile * LANES : half + (tile + 1) * LANES]
         )
-        for tile in range(tiles):
-            z_scr[tile, at : at + rows.shape[0]] = (
-                z[:, tile * LANES : (tile + 1) * LANES]
-                + z[:, half + tile * LANES : half + (tile + 1) * LANES]
-            )
-
-    loads[2].wait()
-    transform(h_scr[...], v_rows)
-    loads[3].wait()
-    transform(x_scr[...].reshape(v_rows, x_scr.shape[2]), 0)
 
     first = my_frq == 0
 
@@ -147,20 +154,17 @@
     mine.start()
     pl.semaphore_wait(barrier, n_dev - 1)
 
-    def send(step, carry):
-        dest = lax.rem(me + step, n_dev)
-        to_inp = dest // n_frq
+    def send(to_inp, to_frq):
         pltpu.make_async_remote_copy(
             src_ref=msg_scr.at[pl.ds(pl.multiple_of(to_inp * msg_rows, SUBL), msg_rows)],
             dst_ref=my_slot,
             send_sem=send_sem,
             recv_sem=recv_sem,
-            device_id=(to_inp, dest % n_frq),
+            device_id=(to_inp, to_frq),
             device_id_type=MESH,
         ).start()
-        return carry
-
-    lax.fori_loop(1, n_dev, send, 0)
+
+    to_others(n_inp, n_frq, my_inp, my_frq, send)
     everything = pltpu.make_async_remote_copy(
         src_ref=out_hbm.at[pl.ds(0, (n_dev - 1) * msg_rows)],
         dst_ref=out_hbm.at[pl.ds(0, (n_dev - 1) * msg_rows)],
@@ -175,8 +179,8 @@
     everything.wait_send()
 
 
-def gram_kernel(cfg, msg_hbm, out_hbm, msg_scr, spec_ref, vis_scr, in_sem, out_sem):
-    n_inp, n_frq, n_loc, n_q, msg_rows, row_block, total_frames, rows_dev = cfg
+def gram_kernel(cfg, msg_hbm, out_hbm, msg_scr, spec_ref, left_scr, vis_scr, in_sem, out_sem):
+    n_inp, n_frq, n_loc, n_q, msg_rows, total_frames, rows_dev = cfg
     depth, inputs = spec_ref.shape
     per_lane = LANES // n_loc
     load = pltpu.make_async_copy(msg_hbm, msg_scr, in_sem)
@@ -216,38 +220,41 @@
                 at = (pair * per_lane + c) * msg_rows
                 spec_ref[at : at + msg_rows, m * LANES : (m + 1) * LANES] = total
 
-    h, m, l = split_bf16(spec_ref[...], 3)
-    right = jnp.concatenate([h, m, h, l, h, m], axis=0)
-    anchor = lax.axis_index("frq") * rows_dev
+    spectra = spec_ref[...]
+    h, m, l = split_bf16(spectra, 3)
+    spare = [jnp.zeros_like(h)] * (-6 % (LANES // depth) if LANES % depth == 0 else 0)
+    right = jnp.concatenate([h, m, h, l, h, m] + spare, axis=0)
+    anchor = pl.multiple_of(lax.axis_index("frq") * rows_dev, LANES)
+    left = spec_ref[:, pl.ds(anchor, rows_dev)] * (1.0 / total_frames)
+    row_at = lax.broadcasted_iota(jnp.int32, (msg_rows, rows_dev), 0)
+    swapped = jnp.concatenate(
+        [
+            jnp.where(
+                row_at < n_q,
+                pltpu.roll(left[at : at + msg_rows], msg_rows - n_q, 0),
+                -pltpu.roll(left[at : at + msg_rows], n_q, 0),
+            )
+            for at in range(0, depth, msg_rows)
+        ],
+        axis=0,
+    )
+    h, m, l = split_bf16(jnp.concatenate([left, swapped], axis=1), 3)
+    left_scr[...] = jnp.concatenate([h, h, m, h, l, m] + spare, axis=0).T
+    width = 2 * LANES
     copies = []
-    for step in range(rows_dev // row_block):
-        start = pl.multiple_of(anchor + step * row_block, LANES)
-        left = spec_ref[:, pl.ds(start, row_block)] * (1.0 / total_frames)
-        row = lax.broadcasted_iota(jnp.int32, left.shape, 0) % msg_rows
-        swapped = jnp.concatenate(
-            [
-                jnp.where(
-                    row[:msg_rows] < n_q,
-                    pltpu.roll(left[at : at + msg_rows], msg_rows - n_q, 0),
-                    -pltpu.roll(left[at : at + msg_rows], n_q, 0),
-                )
-                for at in range(0, depth, msg_rows)
-            ],
-            axis=0,
+    for block in range(inputs // width):
+        vis = jnp.dot(
+            left_scr[...],
+            right[:, block * width : (block + 1) * width],
+            preferred_element_type=jnp.float32,
         )
-        for part, side in enumerate((left, swapped)):
-            h, m, l = split_bf16(side, 3)
-            stack = jnp.concatenate([h, h, m, h, l, m], axis=0)
-            vis = lax.dot_general(
-                stack, right, (((0,), (0,)), ((), ())), preferred_element_type=jnp.float32
-            )
-            rows = pl.ds(step * row_block, row_block)
-            for tile in range(inputs // LANES):
-                at = 2 * tile + part
-                vis_scr[at, rows, :] = vis[:, tile * LANES : (tile + 1) * LANES]
-                copy = pltpu.make_async_copy(
-                    vis_scr.at[at, rows], out_hbm.at[rows, at], out_sem.at[len(copies)]
-                )
+        for tile in range(2):
+            for part in range(2):
+                at = 2 * (2 * block + tile) + part
+                vis_scr[at] = vis[
+                    part * rows_dev : (part + 1) * rows_dev, tile * LANES : (tile + 1) * LANES
+                ]
+                copy = pltpu.make_async_copy(vis_scr.at[at], out_hbm.at[:, at], out_sem.at[at])
                 copy.start()
                 copies.append(copy)
     for copy in copies:
@@ -295,12 +302,12 @@
     )(voltages, h, table, window)
 
     rows_dev = inputs // n_frq
-    row_block = min(LANES, rows_dev)
+    stack = 6 * depth if LANES % depth else -(-6 * depth // LANES) * LANES
     per_row = 2 * inputs // LANES
     vis = pl.pallas_call(
         functools.partial(
             gram_kernel,
-            (n_inp, n_frq, n_loc, n_q, msg_rows, row_block, frames * n_frq, rows_dev),
+            (n_inp, n_frq, n_loc, n_q, msg_rows, frames * n_frq, rows_dev),
         ),
         out_shape=jax.ShapeDtypeStruct((rows_dev, per_row, LANES), jnp.float32),
         in_specs=[pl.BlockSpec(memory_space=pl.ANY)],
@@ -308,9 +315,10 @@
         scratch_shapes=[
             pltpu.VMEM((n_dev * msg_rows, LANES), jnp.float32),
             pltpu.VMEM((depth, inputs), jnp.float32),
+            pltpu.VMEM((2 * rows_dev, stack), jnp.bfloat16),
             pltpu.VMEM((per_row, rows_dev, LANES), jnp.float32),
             pltpu.SemaphoreType.DMA,
-            pltpu.SemaphoreType.DMA((rows_dev // row_block * per_row,)),
+            pltpu.SemaphoreType.DMA((per_row,)),
         ],
         compiler_params=pltpu.CompilerParams(vmem_limit_bytes=60 * 2**20),
         name="gram",

time: 15.5 us -> 16 us (1.032)
  Pallas kernels: 15.3 us -> 15.8 us
    pallas_call x1, Pallas kernels: 11.6 us -> 12.3 us  [body(): pl.pallas_call(functools.partial(spectra_kernel, (n_inp, n_frq, n_loc, fr...]
    pallas_call x1, Pallas kernels: 3.74 us -> 3.53 us  [body(): pl.pallas_call(functools.partial(gram_kernel, (n_inp, n_frq, n_loc, n_q,...]
where the time goes in v4:
time: 16 us; the launch traced here: 15.8 us
  Pallas kernels  15.8 us (99%)
    pallas_call x1, Pallas kernels, body(): pl.pallas_call(functools.partial(spectra_kernel, (n_inp, n_frq, n_loc, fr...  12.3 us
    pallas_call x1, Pallas kernels, body(): pl.pallas_call(functools.partial(gram_kernel, (n_inp, n_frq, n_loc, n_q,...  3.53 us

profile of v4, /device:TPU:0, one launch (start us, length us, event | category | flops | bytes accessed | tf_op | source)
XLA Modules:
  0.0 15.8 jit_solution(5803715747870548555)
XLA Ops:
  0.0 12.3 %spectra_exchange.1.msg_hbm = f32[256,128]{1,0:T(8,128)} custom-call(bf16[64,4,2048]{2,1,0:T(4,128)(2,1)} %x_hbm.1, bf16[192,2048]{1,0:T(8,128)(2,1)} %bitcast.8, f32[32,2048]{1,0:T(8,128)} %constant.2.clone.table_hbm, f32[4,2048]{1,0:T(4,128)} %window_hbm.1), custom_call_target="tpu_custom_call" | custom-call | tf_op jit(solution)/shard_map/spectra_exchange/pallas_call | solution.py:279
  12.3 3.5 %gram.1 = f32[512,16,128]{2,1,0:T(8,128)} custom-call(f32[256,128]{1,0:T(8,128)} %spectra_exchange.1.msg_hbm), custom_call_target="tpu_custom_call" | custom-call | tf_op jit(solution)/shard_map/gram/pallas_call | solution.py:307

commit v5 on v4

--- a/solution.py
+++ b/solution.py
@@ -112,6 +112,7 @@
     lane_group = lax.broadcasted_iota(jnp.int32, (n_loc, LANES), 1) // group
     per_lane = LANES // n_loc
     n_q = 2 * frames // per_lane
+    half_q = n_q // 2
     msg_rows = msg_scr.shape[0] // channels
 
     def frame_products(tile, t):
@@ -135,9 +136,10 @@
         for part in range(2):
             for jb in range(channels // SUBL):
                 row = part * channels + jb * SUBL
-                msg_scr[
-                    pl.ds(jb * SUBL * msg_rows + part * n_q + q, SUBL, stride=msg_rows), :
-                ] = acc[row : row + SUBL]
+                at = q // half_q * n_q + part * half_q + q % half_q
+                msg_scr[pl.ds(jb * SUBL * msg_rows + at, SUBL, stride=msg_rows), :] = acc[
+                    row : row + SUBL
+                ]
     if msg_rows > 2 * n_q:
         for row in range(2 * n_q, msg_rows):
             for jb in range(channels // SUBL):
@@ -145,41 +147,52 @@
                     (SUBL, LANES), jnp.float32
                 )
 
-    my_slot = out_hbm.at[pl.ds(pl.multiple_of(me * msg_rows, SUBL), msg_rows)]
-    mine = pltpu.make_async_copy(
-        msg_scr.at[pl.ds(pl.multiple_of(my_inp * msg_rows, SUBL), msg_rows)],
-        my_slot,
-        in_sem.at[4],
-    )
-    mine.start()
+    own_rows = n_q if n_q % 4 == 0 else msg_rows
+
+    def exchange(rows, waited):
+        my_slot = out_hbm.at[pl.ds(pl.multiple_of(me * msg_rows, SUBL), rows)]
+
+        def message(to_inp):
+            return msg_scr.at[pl.ds(pl.multiple_of(to_inp * msg_rows, SUBL), rows)]
+
+        def send(to_inp, to_frq):
+            pltpu.make_async_remote_copy(
+                src_ref=message(to_inp),
+                dst_ref=my_slot,
+                send_sem=send_sem,
+                recv_sem=recv_sem,
+                device_id=(to_inp, to_frq),
+                device_id_type=MESH,
+            ).start()
+
+        def bytes_of(count):
+            return pltpu.make_async_remote_copy(
+                src_ref=out_hbm.at[pl.ds(0, count)],
+                dst_ref=out_hbm.at[pl.ds(0, count)],
+                send_sem=send_sem,
+                recv_sem=recv_sem,
+                device_id=(my_inp, my_frq),
+                device_id_type=MESH,
+            )
+
+        mine = pltpu.make_async_copy(message(my_inp), my_slot, in_sem.at[4])
+        mine.start()
+        to_others(n_inp, n_frq, my_inp, my_frq, send)
+        bytes_of(waited).wait_recv()
+        bytes_of((n_dev - 1) * rows).wait_send()
+        mine.wait()
+
     pl.semaphore_wait(barrier, n_dev - 1)
-
-    def send(to_inp, to_frq):
-        pltpu.make_async_remote_copy(
-            src_ref=msg_scr.at[pl.ds(pl.multiple_of(to_inp * msg_rows, SUBL), msg_rows)],
-            dst_ref=my_slot,
-            send_sem=send_sem,
-            recv_sem=recv_sem,
-            device_id=(to_inp, to_frq),
-            device_id_type=MESH,
-        ).start()
-
-    to_others(n_inp, n_frq, my_inp, my_frq, send)
-    everything = pltpu.make_async_remote_copy(
-        src_ref=out_hbm.at[pl.ds(0, (n_dev - 1) * msg_rows)],
-        dst_ref=out_hbm.at[pl.ds(0, (n_dev - 1) * msg_rows)],
-        send_sem=send_sem,
-        recv_sem=recv_sem,
-        device_id=(my_inp, my_frq),
-        device_id_type=MESH,
-    )
-    everything.wait_recv()
-
-    mine.wait()
-    everything.wait_send()
-
-
-def gram_kernel(cfg, msg_hbm, out_hbm, msg_scr, spec_ref, left_scr, vis_scr, in_sem, out_sem):
+    arriving = n_inp * ((n_frq - 1) * msg_rows + own_rows)
+    last = my_frq == n_frq - 1
+    pl.when(last)(lambda: exchange(own_rows, arriving - own_rows))
+    pl.when(jnp.logical_not(last))(lambda: exchange(msg_rows, arriving - msg_rows))
+
+
+def gram_kernel(
+    cfg, msg_hbm, out_hbm, msg_scr, spec_ref, left_scr, right_scr, vis_scr,
+    in_sem, out_sem,
+):
     n_inp, n_frq, n_loc, n_q, msg_rows, total_frames, rows_dev = cfg
     depth, inputs = spec_ref.shape
     per_lane = LANES // n_loc
@@ -188,8 +201,8 @@
     load.wait()
 
     row = lax.broadcasted_iota(jnp.int32, (msg_rows, LANES), 0)
-    own = (row % n_q < n_q // 2) & (row < 2 * n_q)
-    later = (row % n_q >= n_q // 2) & (row < 2 * n_q)
+    own = row < n_q
+    later = (row >= n_q) & (row < 2 * n_q)
     lane_part = lax.broadcasted_iota(jnp.int32, (msg_rows, LANES), 1) // n_loc
 
     for m in range(n_inp // per_lane):
@@ -210,12 +223,11 @@
                     piece = pltpu.roll(msgs[f][e], turn, 1) if turn else msgs[f][e]
                     tile = piece if tile is None else jnp.where(lane_part == e, piece, tile)
                 lined.append(tile)
-            shift = n_q // 2
             for pair in range(n_frq // 2):
                 even, odd = lined[2 * pair], lined[2 * pair + 1]
-                total = even + jnp.where(later, pltpu.roll(odd, shift, 0), 0.0)
+                total = even + jnp.where(later, pltpu.roll(odd, n_q, 0), 0.0)
                 if pair:
-                    before = pltpu.roll(lined[2 * pair - 1], msg_rows - shift, 0)
+                    before = pltpu.roll(lined[2 * pair - 1], msg_rows - n_q, 0)
                     total = total + jnp.where(own, before, 0.0)
                 at = (pair * per_lane + c) * msg_rows
                 spec_ref[at : at + msg_rows, m * LANES : (m + 1) * LANES] = total
@@ -230,9 +242,9 @@
     swapped = jnp.concatenate(
         [
             jnp.where(
-                row_at < n_q,
-                pltpu.roll(left[at : at + msg_rows], msg_rows - n_q, 0),
-                -pltpu.roll(left[at : at + msg_rows], n_q, 0),
+                row_at % n_q < n_q // 2,
+                pltpu.roll(left[at : at + msg_rows], msg_rows - n_q // 2, 0),
+                -pltpu.roll(left[at : at + msg_rows], n_q // 2, 0),
             )
             for at in range(0, depth, msg_rows)
         ],
@@ -240,25 +252,35 @@
     )
     h, m, l = split_bf16(jnp.concatenate([left, swapped], axis=1), 3)
     left_scr[...] = jnp.concatenate([h, h, m, h, l, m] + spare, axis=0).T
-    width = 2 * LANES
-    copies = []
-    for block in range(inputs // width):
+    right_scr[...] = right
+    per_row = 2 * inputs // LANES
+    block = SUBL * SUBL
+    blocks = rows_dev // block
+
+    def out_copy(step):
+        rows = pl.ds(pl.multiple_of(step * block * per_row, block * per_row), block * per_row)
+        return pltpu.make_async_copy(vis_scr.at[rows], out_hbm.at[rows], out_sem.at[step])
+
+    def one_block(step, carry):
+        row = pl.multiple_of(step * block, block)
+        sides = [left_scr[pl.ds(part * rows_dev + row, block), :] for part in range(2)]
         vis = jnp.dot(
-            left_scr[...],
-            right[:, block * width : (block + 1) * width],
-            preferred_element_type=jnp.float32,
+            jnp.concatenate(sides, axis=0), right_scr[...], preferred_element_type=jnp.float32
         )
-        for tile in range(2):
-            for part in range(2):
-                at = 2 * (2 * block + tile) + part
-                vis_scr[at] = vis[
-                    part * rows_dev : (part + 1) * rows_dev, tile * LANES : (tile + 1) * LANES
-                ]
-                copy = pltpu.make_async_copy(vis_scr.at[at], out_hbm.at[:, at], out_sem.at[at])
-                copy.start()
-                copies.append(copy)
-    for copy in copies:
-        copy.wait()
+        for part in range(2):
+            for r in range(0, block, SUBL):
+                for tile in range(inputs // LANES):
+                    at = (row + r) * per_row + 2 * tile + part
+                    vis_scr[pl.ds(at, SUBL, stride=per_row), :] = vis[
+                        part * block + r : part * block + r + SUBL,
+                        tile * LANES : (tile + 1) * LANES,
+                    ]
+        out_copy(step).start()
+        return carry
+
+    lax.fori_loop(0, blocks, one_block, 0)
+    for step in range(blocks):
+        out_copy(step).wait()
 
 
 def body(n_inp, n_frq, voltages, history, window):
@@ -309,16 +331,17 @@
             gram_kernel,
             (n_inp, n_frq, n_loc, n_q, msg_rows, frames * n_frq, rows_dev),
         ),
-        out_shape=jax.ShapeDtypeStruct((rows_dev, per_row, LANES), jnp.float32),
+        out_shape=jax.ShapeDtypeStruct((rows_dev * per_row, LANES), jnp.float32),
         in_specs=[pl.BlockSpec(memory_space=pl.ANY)],
         out_specs=pl.BlockSpec(memory_space=pl.ANY),
         scratch_shapes=[
             pltpu.VMEM((n_dev * msg_rows, LANES), jnp.float32),
             pltpu.VMEM((depth, inputs), jnp.float32),
             pltpu.VMEM((2 * rows_dev, stack), jnp.bfloat16),
-            pltpu.VMEM((per_row, rows_dev, LANES), jnp.float32),
+            pltpu.VMEM((stack, inputs), jnp.bfloat16),
+            pltpu.VMEM((rows_dev * per_row, LANES), jnp.float32),
             pltpu.SemaphoreType.DMA,
-            pltpu.SemaphoreType.DMA((per_row,)),
+            pltpu.SemaphoreType.DMA((rows_dev // (SUBL * SUBL),)),
         ],
         compiler_params=pltpu.CompilerParams(vmem_limit_bytes=60 * 2**20),
         name="gram",

time: 16 us -> 16 us (level)
    pallas_call x1, Pallas kernels: 3.53 us -> 4.28 us  [body(): pl.pallas_call(functools.partial(gram_kernel, (n_inp, n_frq, n_loc, n_q,...]
    pallas_call x1, Pallas kernels: 12.3 us -> 11.5 us  [body(): pl.pallas_call(functools.partial(spectra_kernel, (n_inp, n_frq, n_loc, fr...]
where the time goes in v5:
time: 16 us; the launch traced here: 15.8 us
  Pallas kernels  15.8 us (99%)
    pallas_call x1, Pallas kernels, body(): pl.pallas_call(functools.partial(spectra_kernel, (n_inp, n_frq, n_loc, fr...  11.5 us
    pallas_call x1, Pallas kernels, body(): pl.pallas_call(functools.partial(gram_kernel, (n_inp, n_frq, n_loc, n_q,...  4.28 us

profile of v5, /device:TPU:0, one launch (start us, length us, event | category | flops | bytes accessed | tf_op | source)
XLA Modules:
  0.0 15.8 jit_solution(13168531062750640080)
XLA Ops:
  0.0 11.5 %spectra_exchange.1.msg_hbm = f32[256,128]{1,0:T(8,128)} custom-call(bf16[64,4,2048]{2,1,0:T(4,128)(2,1)} %x_hbm.1, bf16[192,2048]{1,0:T(8,128)(2,1)} %bitcast.8, f32[32,2048]{1,0:T(8,128)} %constant.2.clone.table_hbm, f32[4,2048]{1,0:T(4,128)} %window_hbm.1), custom_call_target="tpu_custom_call" | custom-call | tf_op jit(solution)/shard_map/spectra_exchange/pallas_call | solution.py:301
  11.6 4.3 %gram.1 = f32[8192,128]{1,0:T(8,128)} custom-call(f32[256,128]{1,0:T(8,128)} %spectra_exchange.1.msg_hbm), custom_call_target="tpu_custom_call" | custom-call | tf_op jit(solution)/shard_map/gram/pallas_call | solution.py:329

commit v6 on v4

--- a/solution.py
+++ b/solution.py
@@ -33,30 +33,21 @@
     return out
 
 
-def to_others(n_inp, n_frq, my_inp, my_frq, act):
-    def group(ahead, low):
-        to_inp = lax.rem(my_inp + ahead, n_inp)
-        for turn in range(low, n_frq):
-            act(to_inp, lax.rem(my_frq + turn, n_frq))
-
-    if n_inp * n_frq <= 32:
-        for step in range(n_inp - 1):
-            group((n_inp // 2 + step) % n_inp if step < n_inp // 2 else n_inp - 1 - step, 0)
-    else:
-        lax.fori_loop(1, n_inp, lambda step, carry: (group(step, 0), carry)[1], 0)
-    group(0, 1)
-
-
 def spectra_kernel(
     cfg, x_hbm, h_hbm, table_hbm, window_hbm, out_hbm,
-    x_scr, h_scr, table_scr, window_scr, mat_scr, z_scr, msg_scr,
-    in_sem, send_sem, recv_sem,
+    x_scr, h_scr, table_scr, window_scr, mat_scr, z_scr, msg_scr, group_scr, tile_scr,
+    in_sem, near_send, near_recv, send_sem, recv_sem,
 ):
     n_inp, n_frq, n_loc, frames, taps, channels = cfg
-    n_dev = n_inp * n_frq
     my_inp = lax.axis_index("inp")
     my_frq = lax.axis_index("frq")
-    me = my_inp * n_frq + my_frq
+    per_lane = LANES // n_loc
+    members = per_lane * n_frq
+    share = channels // members
+    member = lax.rem(my_inp, per_lane) * n_frq + my_frq
+    my_group = my_inp // per_lane
+    owner = my_inp // (CH_DEV * share)
+    owns_mine = owner == member
     v_rows = n_loc * frames
     loads = [
         pltpu.make_async_copy(table_hbm, table_scr, in_sem.at[0]),
@@ -72,7 +63,19 @@
     def greet(to_inp, to_frq):
         pl.semaphore_signal(barrier, inc=1, device_id=(to_inp, to_frq), device_id_type=MESH)
 
-    to_others(n_inp, n_frq, my_inp, my_frq, greet)
+    def at_member(index):
+        return my_group * per_lane + index // n_frq, lax.rem(index, n_frq)
+
+    for turn in range(1, members):
+        greet(*at_member(lax.rem(member + turn, members)))
+    n_groups = n_inp // per_lane
+    for turn in range(n_groups):
+        group_at = lax.rem(my_group + turn, n_groups)
+        sender = (group_at * per_lane + owner // n_frq, lax.rem(owner, n_frq))
+        if turn:
+            greet(*sender)
+        else:
+            pl.when(jnp.logical_not(owns_mine))(functools.partial(greet, *sender))
 
     loads[0].wait()
     loads[1].wait()
@@ -110,8 +113,8 @@
     held = {(tile, u): frame(tile, u) for tile in range(tiles) for u in range(1 - taps, frames)}
     per_tile = LANES // group
     lane_group = lax.broadcasted_iota(jnp.int32, (n_loc, LANES), 1) // group
-    per_lane = LANES // n_loc
     n_q = 2 * frames // per_lane
+    half_q = n_q // 2
     msg_rows = msg_scr.shape[0] // channels
 
     def frame_products(tile, t):
@@ -135,9 +138,10 @@
         for part in range(2):
             for jb in range(channels // SUBL):
                 row = part * channels + jb * SUBL
-                msg_scr[
-                    pl.ds(jb * SUBL * msg_rows + part * n_q + q, SUBL, stride=msg_rows), :
-                ] = acc[row : row + SUBL]
+                at = q // half_q * n_q + part * half_q + q % half_q
+                msg_scr[pl.ds(jb * SUBL * msg_rows + at, SUBL, stride=msg_rows), :] = acc[
+                    row : row + SUBL
+                ]
     if msg_rows > 2 * n_q:
         for row in range(2 * n_q, msg_rows):
             for jb in range(channels // SUBL):
@@ -145,18 +149,72 @@
                     (SUBL, LANES), jnp.float32
                 )
 
-    my_slot = out_hbm.at[pl.ds(pl.multiple_of(me * msg_rows, SUBL), msg_rows)]
-    mine = pltpu.make_async_copy(
-        msg_scr.at[pl.ds(pl.multiple_of(my_inp * msg_rows, SUBL), msg_rows)],
-        my_slot,
-        in_sem.at[4],
-    )
-    mine.start()
-    pl.semaphore_wait(barrier, n_dev - 1)
-
-    def send(to_inp, to_frq):
+    greeted = members - 1 + share * n_frq - owns_mine.astype(jnp.int32)
+    pl.semaphore_wait(barrier, greeted)
+
+    def wait_for(ref, rows, sends, receives):
+        return pltpu.make_async_remote_copy(
+            src_ref=ref.at[pl.ds(0, rows)],
+            dst_ref=ref.at[pl.ds(0, rows)],
+            send_sem=sends,
+            recv_sem=receives,
+            device_id=(my_inp, my_frq),
+            device_id_type=MESH,
+        )
+
+    span = share * msg_rows
+    mine = group_scr.at[pl.ds(pl.multiple_of(member * span, SUBL), span)]
+    for turn in range(1, members):
+        index = lax.rem(member + turn, members)
         pltpu.make_async_remote_copy(
-            src_ref=msg_scr.at[pl.ds(pl.multiple_of(to_inp * msg_rows, SUBL), msg_rows)],
+            src_ref=msg_scr.at[pl.ds(pl.multiple_of(index * span, SUBL), span)],
+            dst_ref=mine,
+            send_sem=near_send,
+            recv_sem=near_recv,
+            device_id=at_member(index),
+            device_id_type=MESH,
+        ).start()
+    group_scr[pl.ds(pl.multiple_of(member * span, SUBL), span), :] = msg_scr[
+        pl.ds(pl.multiple_of(member * span, SUBL), span), :
+    ]
+    near = wait_for(group_scr, (members - 1) * span, near_send, near_recv)
+    near.wait_recv()
+
+    row = lax.broadcasted_iota(jnp.int32, (msg_rows, LANES), 0)
+    own = row < n_q
+    later = (row >= n_q) & (row < 2 * n_q)
+    lane_part = lax.broadcasted_iota(jnp.int32, (msg_rows, LANES), 1) // n_loc
+    depth = (n_frq // 2) * per_lane * msg_rows
+    my_slot = out_hbm.at[pl.ds(pl.multiple_of(my_group * depth, SUBL), depth)]
+    for ch in range(share):
+        for c in range(per_lane):
+            lined = []
+            for f in range(n_frq):
+                tile = None
+                for e in range(per_lane):
+                    at = (e * n_frq + f) * span + ch * msg_rows
+                    piece = group_scr[at : at + msg_rows, :]
+                    turn = (e - c) * n_loc % LANES
+                    piece = pltpu.roll(piece, turn, 1) if turn else piece
+                    tile = piece if tile is None else jnp.where(lane_part == e, piece, tile)
+                lined.append(tile)
+            for pair in range(n_frq // 2):
+                even, odd = lined[2 * pair], lined[2 * pair + 1]
+                total = even + jnp.where(later, pltpu.roll(odd, n_q, 0), 0.0)
+                if pair:
+                    before = pltpu.roll(lined[2 * pair - 1], msg_rows - n_q, 0)
+                    total = total + jnp.where(own, before, 0.0)
+                at = ch * depth + (pair * per_lane + c) * msg_rows
+                tile_scr[at : at + msg_rows, :] = total
+
+    def keep(ch):
+        pltpu.make_async_copy(
+            tile_scr.at[pl.ds(ch * depth, depth)], my_slot, in_sem.at[4]
+        ).start()
+
+    def send(ch, to_inp, to_frq):
+        pltpu.make_async_remote_copy(
+            src_ref=tile_scr.at[pl.ds(ch * depth, depth)],
             dst_ref=my_slot,
             send_sem=send_sem,
             recv_sem=recv_sem,
@@ -164,62 +222,38 @@
             device_id_type=MESH,
         ).start()
 
-    to_others(n_inp, n_frq, my_inp, my_frq, send)
-    everything = pltpu.make_async_remote_copy(
-        src_ref=out_hbm.at[pl.ds(0, (n_dev - 1) * msg_rows)],
-        dst_ref=out_hbm.at[pl.ds(0, (n_dev - 1) * msg_rows)],
-        send_sem=send_sem,
-        recv_sem=recv_sem,
-        device_id=(my_inp, my_frq),
-        device_id_type=MESH,
-    )
-    everything.wait_recv()
-
-    mine.wait()
-    everything.wait_send()
+    for turn in range(n_frq - 1, -1, -1):
+        for ch in range(share):
+            to_inp = member * share + ch
+            to = functools.partial(send, ch, to_inp, lax.rem(my_frq + turn, n_frq))
+            if turn:
+                to()
+            else:
+                pl.when(to_inp != my_inp)(to)
+                pl.when(to_inp == my_inp)(functools.partial(keep, ch))
+    near.wait_send()
+
+    def finish(kept):
+        if kept:
+            pltpu.make_async_copy(
+                tile_scr.at[pl.ds(0, depth)], my_slot, in_sem.at[4]
+            ).wait()
+        wait_for(out_hbm, (n_groups - kept) * depth, send_sem, recv_sem).wait_recv()
+        wait_for(out_hbm, (share * n_frq - kept) * depth, send_sem, recv_sem).wait_send()
+
+    pl.when(owns_mine)(lambda: finish(1))
+    pl.when(jnp.logical_not(owns_mine))(lambda: finish(0))
 
 
 def gram_kernel(cfg, msg_hbm, out_hbm, msg_scr, spec_ref, left_scr, vis_scr, in_sem, out_sem):
-    n_inp, n_frq, n_loc, n_q, msg_rows, total_frames, rows_dev = cfg
+    n_q, msg_rows, total_frames, rows_dev = cfg
     depth, inputs = spec_ref.shape
-    per_lane = LANES // n_loc
     load = pltpu.make_async_copy(msg_hbm, msg_scr, in_sem)
     load.start()
     load.wait()
 
-    row = lax.broadcasted_iota(jnp.int32, (msg_rows, LANES), 0)
-    own = (row % n_q < n_q // 2) & (row < 2 * n_q)
-    later = (row % n_q >= n_q // 2) & (row < 2 * n_q)
-    lane_part = lax.broadcasted_iota(jnp.int32, (msg_rows, LANES), 1) // n_loc
-
-    for m in range(n_inp // per_lane):
-        msgs = [
-            [
-                msg_scr[((m * per_lane + e) * n_frq + f) * msg_rows :
-                         ((m * per_lane + e) * n_frq + f + 1) * msg_rows, :]
-                for e in range(per_lane)
-            ]
-            for f in range(n_frq)
-        ]
-        for c in range(per_lane):
-            lined = []
-            for f in range(n_frq):
-                tile = None
-                for e in range(per_lane):
-                    turn = (e - c) * n_loc % LANES
-                    piece = pltpu.roll(msgs[f][e], turn, 1) if turn else msgs[f][e]
-                    tile = piece if tile is None else jnp.where(lane_part == e, piece, tile)
-                lined.append(tile)
-            shift = n_q // 2
-            for pair in range(n_frq // 2):
-                even, odd = lined[2 * pair], lined[2 * pair + 1]
-                total = even + jnp.where(later, pltpu.roll(odd, shift, 0), 0.0)
-                if pair:
-                    before = pltpu.roll(lined[2 * pair - 1], msg_rows - shift, 0)
-                    total = total + jnp.where(own, before, 0.0)
-                at = (pair * per_lane + c) * msg_rows
-                spec_ref[at : at + msg_rows, m * LANES : (m + 1) * LANES] = total
-
+    for tile in range(inputs // LANES):
+        spec_ref[:, tile * LANES : (tile + 1) * LANES] = msg_scr[tile * depth : (tile + 1) * depth]
     spectra = spec_ref[...]
     h, m, l = split_bf16(spectra, 3)
     spare = [jnp.zeros_like(h)] * (-6 % (LANES // depth) if LANES % depth == 0 else 0)
@@ -230,9 +264,9 @@
     swapped = jnp.concatenate(
         [
             jnp.where(
-                row_at < n_q,
-                pltpu.roll(left[at : at + msg_rows], msg_rows - n_q, 0),
-                -pltpu.roll(left[at : at + msg_rows], n_q, 0),
+                row_at % n_q < n_q // 2,
+                pltpu.roll(left[at : at + msg_rows], msg_rows - n_q // 2, 0),
+                -pltpu.roll(left[at : at + msg_rows], n_q // 2, 0),
             )
             for at in range(0, depth, msg_rows)
         ],
@@ -274,13 +308,14 @@
     msg_rows = -(-2 * n_q // SUBL) * SUBL
     depth = (n_frq // 2) * per_lane * msg_rows
     x_rows = n_loc * (frames + taps - 1)
-    n_dev = n_inp * n_frq
+    n_groups = n_inp // per_lane
+    members = per_lane * n_frq
     half = taps * 2 * channels
     spectra = pl.pallas_call(
         functools.partial(
             spectra_kernel, (n_inp, n_frq, n_loc, frames, taps, channels)
         ),
-        out_shape=jax.ShapeDtypeStruct((n_dev * msg_rows, LANES), jnp.float32),
+        out_shape=jax.ShapeDtypeStruct((n_groups * depth, LANES), jnp.float32),
         in_specs=[pl.BlockSpec(memory_space=pl.ANY)] * 4,
         out_specs=pl.BlockSpec(memory_space=pl.ANY),
         scratch_shapes=[
@@ -291,7 +326,11 @@
             pltpu.VMEM((2 * half, samples), jnp.bfloat16),
             pltpu.VMEM((half // LANES, x_rows, LANES), jnp.float32),
             pltpu.VMEM((channels * msg_rows, LANES), jnp.float32),
+            pltpu.VMEM((channels * msg_rows, LANES), jnp.float32),
+            pltpu.VMEM((channels // members * depth, LANES), jnp.float32),
             pltpu.SemaphoreType.DMA((5,)),
+            pltpu.SemaphoreType.DMA,
+            pltpu.SemaphoreType.DMA,
             pltpu.SemaphoreType.DMA,
             pltpu.SemaphoreType.DMA,
         ],
@@ -307,13 +346,13 @@
     vis = pl.pallas_call(
         functools.partial(
             gram_kernel,
-            (n_inp, n_frq, n_loc, n_q, msg_rows, frames * n_frq, rows_dev),
+            (n_q, msg_rows, frames * n_frq, rows_dev),
         ),
         out_shape=jax.ShapeDtypeStruct((rows_dev, per_row, LANES), jnp.float32),
         in_specs=[pl.BlockSpec(memory_space=pl.ANY)],
         out_specs=pl.BlockSpec(memory_space=pl.ANY),
         scratch_shapes=[
-            pltpu.VMEM((n_dev * msg_rows, LANES), jnp.float32),
+            pltpu.VMEM((n_groups * depth, LANES), jnp.float32),
             pltpu.VMEM((depth, inputs), jnp.float32),
             pltpu.VMEM((2 * rows_dev, stack), jnp.bfloat16),
             pltpu.VMEM((per_row, rows_dev, LANES), jnp.float32),

time: 16 us -> 17.6 us (1.10)
  Pallas kernels: 15.8 us -> 17.4 us
    pallas_call x1, Pallas kernels: 12.3 us -> 14 us  [body(): pl.pallas_call(functools.partial(spectra_kernel, (n_inp, n_frq, n_loc, fr...]
where the time goes in v6:
time: 17.6 us; the launch traced here: 17.4 us
  Pallas kernels  17.4 us (99%)
    pallas_call x1, Pallas kernels, body(): pl.pallas_call(functools.partial(spectra_kernel, (n_inp, n_frq, n_loc, fr...  14 us
    pallas_call x1, Pallas kernels, body(): pl.pallas_call(functools.partial(gram_kernel, (n_q, msg_rows, frames * n_...  3.4 us

profile of v6, /device:TPU:0, one launch (start us, length us, event | category | flops | bytes accessed | tf_op | source)
XLA Modules:
  0.0 17.4 jit_solution(16685251721742095142)
XLA Ops:
  0.0 14.0 %spectra_exchange.1.msg_hbm = f32[128,128]{1,0:T(8,128)} custom-call(bf16[64,4,2048]{2,1,0:T(4,128)(2,1)} %x_hbm.1, bf16[192,2048]{1,0:T(8,128)(2,1)} %bitcast.8, f32[32,2048]{1,0:T(8,128)} %constant.2.clone.table_hbm, f32[4,2048]{1,0:T(4,128)} %window_hbm.1), custom_call_target="tpu_custom_call" | custom-call | tf_op jit(solution)/shard_map/spectra_exchange/pallas_call | solution.py:314
  14.0 3.4 %gram.1 = f32[512,16,128]{2,1,0:T(8,128)} custom-call(f32[128,128]{1,0:T(8,128)} %spectra_exchange.1.msg_hbm), custom_call_target="tpu_custom_call" | custom-call | tf_op jit(solution)/shard_map/gram/pallas_call | solution.py:346

commit v7 on v5

--- a/solution.py
+++ b/solution.py
@@ -62,7 +62,9 @@
         pltpu.make_async_copy(table_hbm, table_scr, in_sem.at[0]),
         pltpu.make_async_copy(window_hbm, window_scr, in_sem.at[1]),
         pltpu.make_async_copy(h_hbm, h_scr, in_sem.at[2]),
-        pltpu.make_async_copy(x_hbm, x_scr, in_sem.at[3]),
+    ] + [
+        pltpu.make_async_copy(x_hbm.at[:, tile], x_scr.at[tile], in_sem.at[4 + tile])
+        for tile in range(x_hbm.shape[1])
     ]
     for load in loads:
         load.start()
@@ -85,8 +87,11 @@
     tiles = half // LANES
 
     loads[2].wait()
-    loads[3].wait()
-    rows = jnp.concatenate([x_scr[...].reshape(v_rows, x_scr.shape[2]), h_scr[...]], axis=0)
+    for load in loads[3:]:
+        load.wait()
+    flat = x_scr.reshape(x_scr.shape[0], v_rows, LANES)
+    rows = jnp.concatenate([flat[tile] for tile in range(x_scr.shape[0])], axis=1)
+    rows = jnp.concatenate([rows, h_scr[...]], axis=0)
     z = lax.dot_general(
         rows, mat_scr[...], (((1,), (1,)), ((), ())), preferred_element_type=jnp.float32
     )
@@ -175,7 +180,7 @@
                 device_id_type=MESH,
             )
 
-        mine = pltpu.make_async_copy(message(my_inp), my_slot, in_sem.at[4])
+        mine = pltpu.make_async_copy(message(my_inp), my_slot, in_sem.at[3])
         mine.start()
         to_others(n_inp, n_frq, my_inp, my_frq, send)
         bytes_of(waited).wait_recv()
@@ -187,6 +192,12 @@
     last = my_frq == n_frq - 1
     pl.when(last)(lambda: exchange(own_rows, arriving - own_rows))
     pl.when(jnp.logical_not(last))(lambda: exchange(msg_rows, arriving - msg_rows))
+
+
+def row_blocks(rows):
+    small = SUBL * SUBL
+    edges = [0, small] + list(range(2 * small, rows + 1, 2 * small))
+    return [(low, high - low) for low, high in zip(edges, edges[1:])]
 
 
 def gram_kernel(
@@ -254,16 +265,12 @@
     left_scr[...] = jnp.concatenate([h, h, m, h, l, m] + spare, axis=0).T
     right_scr[...] = right
     per_row = 2 * inputs // LANES
-    block = SUBL * SUBL
-    blocks = rows_dev // block
-
-    def out_copy(step):
-        rows = pl.ds(pl.multiple_of(step * block * per_row, block * per_row), block * per_row)
-        return pltpu.make_async_copy(vis_scr.at[rows], out_hbm.at[rows], out_sem.at[step])
-
-    def one_block(step, carry):
-        row = pl.multiple_of(step * block, block)
-        sides = [left_scr[pl.ds(part * rows_dev + row, block), :] for part in range(2)]
+    copies = []
+    for row, block in row_blocks(rows_dev):
+        sides = [
+            left_scr[part * rows_dev + row : part * rows_dev + row + block, :]
+            for part in range(2)
+        ]
         vis = jnp.dot(
             jnp.concatenate(sides, axis=0), right_scr[...], preferred_element_type=jnp.float32
         )
@@ -275,12 +282,13 @@
                         part * block + r : part * block + r + SUBL,
                         tile * LANES : (tile + 1) * LANES,
                     ]
-        out_copy(step).start()
-        return carry
-
-    lax.fori_loop(0, blocks, one_block, 0)
-    for step in range(blocks):
-        out_copy(step).wait()
+        rows = pl.ds(row * per_row, block * per_row)
+        copies.append(
+            pltpu.make_async_copy(vis_scr.at[rows], out_hbm.at[rows], out_sem.at[len(copies)])
+        )
+        copies[-1].start()
+    for copy in copies:
+        copy.wait()
 
 
 def body(n_inp, n_frq, voltages, history, window):
@@ -288,6 +296,7 @@
     taps = window.shape[0]
     inputs = n_loc * n_inp
     channels = CH_DEV * n_inp
+    x = voltages.reshape(n_loc, frames, samples // LANES, LANES).transpose(0, 2, 1, 3)
     h = history.transpose(1, 0, 2).reshape((taps - 1) * n_loc, samples)
     table = jnp.asarray(dft_rows(channels, samples))
 
@@ -306,14 +315,14 @@
         in_specs=[pl.BlockSpec(memory_space=pl.ANY)] * 4,
         out_specs=pl.BlockSpec(memory_space=pl.ANY),
         scratch_shapes=[
-            pltpu.VMEM((n_loc, frames, samples), jnp.bfloat16),
+            pltpu.VMEM((samples // LANES, n_loc, frames, LANES), jnp.bfloat16),
             pltpu.VMEM(((taps - 1) * n_loc, samples), jnp.bfloat16),
             pltpu.VMEM((2 * channels, samples), jnp.float32),
             pltpu.VMEM((taps, samples), jnp.float32),
             pltpu.VMEM((2 * half, samples), jnp.bfloat16),
             pltpu.VMEM((half // LANES, x_rows, LANES), jnp.float32),
             pltpu.VMEM((channels * msg_rows, LANES), jnp.float32),
-            pltpu.SemaphoreType.DMA((5,)),
+            pltpu.SemaphoreType.DMA((4 + samples // LANES,)),
             pltpu.SemaphoreType.DMA,
             pltpu.SemaphoreType.DMA,
         ],
@@ -321,7 +330,7 @@
             collective_id=0, has_side_effects=True, vmem_limit_bytes=60 * 2**20
         ),
         name="spectra_exchange",
-    )(voltages, h, table, window)
+    )(x, h, table, window)
 
     rows_dev = inputs // n_frq
     stack = 6 * depth if LANES % depth else -(-6 * depth // LANES) * LANES
@@ -341,7 +350,7 @@
             pltpu.VMEM((stack, inputs), jnp.bfloat16),
             pltpu.VMEM((rows_dev * per_row, LANES), jnp.float32),
             pltpu.SemaphoreType.DMA,
-            pltpu.SemaphoreType.DMA((rows_dev // (SUBL * SUBL),)),
+            pltpu.SemaphoreType.DMA((len(row_blocks(rows_dev)),)),
         ],
         compiler_params=pltpu.CompilerParams(vmem_limit_bytes=60 * 2**20),
         name="gram",

time: 16 us -> 15.5 us (0.969)
  Pallas kernels: 15.8 us -> 15.3 us
    pallas_call x1, Pallas kernels: 4.28 us -> 3.64 us  [body(): pl.pallas_call(functools.partial(gram_kernel, (n_inp, n_frq, n_loc, n_q,...]
where the time goes in v7:
time: 15.5 us; the launch traced here: 15.3 us
  Pallas kernels  15.3 us (99%)
    pallas_call x1, Pallas kernels, body(): pl.pallas_call(functools.partial(spectra_kernel, (n_inp, n_frq, n_loc, fr...  11.7 us
    pallas_call x1, Pallas kernels, body(): pl.pallas_call(functools.partial(gram_kernel, (n_inp, n_frq, n_loc, n_q,...  3.64 us

profile of v7, /device:TPU:0, one launch (start us, length us, event | category | flops | bytes accessed | tf_op | source)
XLA Modules:
  0.0 15.3 jit_solution(1013959440992524509)
XLA Ops:
  0.0 11.7 %spectra_exchange.1.msg_hbm = f32[256,128]{1,0:T(8,128)} custom-call(bf16[64,16,4,128]{3,2,1,0:T(4,128)(2,1)} %bitcast.11, bf16[192,2048]{1,0:T(8,128)(2,1)} %bitcast.12, f32[32,2048]{1,0:T(8,128)} %constant.2.clone.table_hbm, f32[4,2048]{1,0:T(4,128)} %window_hbm.1), custom_call_target="tpu_custom_call" | custom-call | tf_op jit(solution)/shard_map/spectra_exchange/pallas_call | solution.py:310
  11.7 3.6 %gram.1 = f32[8192,128]{1,0:T(8,128)} custom-call(f32[256,128]{1,0:T(8,128)} %spectra_exchange.1.msg_hbm), custom_call_target="tpu_custom_call" | custom-call | tf_op jit(solution)/shard_map/gram/pallas_call | solution.py:338

commit v8 on v7

--- a/solution.py
+++ b/solution.py
@@ -33,18 +33,14 @@
     return out
 
 
-def to_others(n_inp, n_frq, my_inp, my_frq, act):
-    def group(ahead, low):
+def others(n_inp, n_frq, my_inp, my_frq):
+    found = []
+    for step in range(n_inp):
+        ahead = (n_inp // 2 + step) % n_inp if step < n_inp // 2 else n_inp - 1 - step
         to_inp = lax.rem(my_inp + ahead, n_inp)
-        for turn in range(low, n_frq):
-            act(to_inp, lax.rem(my_frq + turn, n_frq))
-
-    if n_inp * n_frq <= 32:
-        for step in range(n_inp - 1):
-            group((n_inp // 2 + step) % n_inp if step < n_inp // 2 else n_inp - 1 - step, 0)
-    else:
-        lax.fori_loop(1, n_inp, lambda step, carry: (group(step, 0), carry)[1], 0)
-    group(0, 1)
+        for turn in range(0 if ahead else 1, n_frq):
+            found.append((to_inp, lax.rem(my_frq + turn, n_frq)))
+    return found
 
 
 def spectra_kernel(
@@ -71,10 +67,13 @@
 
     barrier = pltpu.get_barrier_semaphore()
 
-    def greet(to_inp, to_frq):
-        pl.semaphore_signal(barrier, inc=1, device_id=(to_inp, to_frq), device_id_type=MESH)
-
-    to_others(n_inp, n_frq, my_inp, my_frq, greet)
+    devices = others(n_inp, n_frq, my_inp, my_frq)
+
+    def greet(some):
+        for device in some:
+            pl.semaphore_signal(barrier, inc=1, device_id=device, device_id_type=MESH)
+
+    greet(devices[: n_dev // 2])
 
     loads[0].wait()
     loads[1].wait()
@@ -83,6 +82,7 @@
         hi, lo = split_bf16(window_scr[tap : tap + 1, :] * table_scr[...], 2)
         mat_scr[tap * group : (tap + 1) * group, :] = hi
         mat_scr[(taps + tap) * group : (taps + tap + 1) * group, :] = lo
+        greet(devices[n_dev // 2 :][tap::taps])
     half = taps * group
     tiles = half // LANES
 
@@ -152,51 +152,39 @@
                     (SUBL, LANES), jnp.float32
                 )
 
-    own_rows = n_q if n_q % 4 == 0 else msg_rows
-
-    def exchange(rows, waited):
-        my_slot = out_hbm.at[pl.ds(pl.multiple_of(me * msg_rows, SUBL), rows)]
-
-        def message(to_inp):
-            return msg_scr.at[pl.ds(pl.multiple_of(to_inp * msg_rows, SUBL), rows)]
-
-        def send(to_inp, to_frq):
-            pltpu.make_async_remote_copy(
-                src_ref=message(to_inp),
-                dst_ref=my_slot,
-                send_sem=send_sem,
-                recv_sem=recv_sem,
-                device_id=(to_inp, to_frq),
-                device_id_type=MESH,
-            ).start()
-
-        def bytes_of(count):
-            return pltpu.make_async_remote_copy(
-                src_ref=out_hbm.at[pl.ds(0, count)],
-                dst_ref=out_hbm.at[pl.ds(0, count)],
-                send_sem=send_sem,
-                recv_sem=recv_sem,
-                device_id=(my_inp, my_frq),
-                device_id_type=MESH,
-            )
-
-        mine = pltpu.make_async_copy(message(my_inp), my_slot, in_sem.at[3])
-        mine.start()
-        to_others(n_inp, n_frq, my_inp, my_frq, send)
-        bytes_of(waited).wait_recv()
-        bytes_of((n_dev - 1) * rows).wait_send()
-        mine.wait()
-
     pl.semaphore_wait(barrier, n_dev - 1)
-    arriving = n_inp * ((n_frq - 1) * msg_rows + own_rows)
-    last = my_frq == n_frq - 1
-    pl.when(last)(lambda: exchange(own_rows, arriving - own_rows))
-    pl.when(jnp.logical_not(last))(lambda: exchange(msg_rows, arriving - msg_rows))
+    my_slot = out_hbm.at[pl.ds(pl.multiple_of(me * msg_rows, SUBL), msg_rows)]
+
+    def message(to_inp):
+        return msg_scr.at[pl.ds(pl.multiple_of(to_inp * msg_rows, SUBL), msg_rows)]
+
+    for device in devices:
+        pltpu.make_async_remote_copy(
+            src_ref=message(device[0]),
+            dst_ref=my_slot,
+            send_sem=send_sem,
+            recv_sem=recv_sem,
+            device_id=device,
+            device_id_type=MESH,
+        ).start()
+    mine = pltpu.make_async_copy(message(my_inp), my_slot, in_sem.at[3])
+    mine.start()
+    rest = out_hbm.at[pl.ds(0, (n_dev - 1) * msg_rows)]
+    everything = pltpu.make_async_remote_copy(
+        src_ref=rest,
+        dst_ref=rest,
+        send_sem=send_sem,
+        recv_sem=recv_sem,
+        device_id=(my_inp, my_frq),
+        device_id_type=MESH,
+    )
+    mine.wait()
+    everything.wait_recv()
+    everything.wait_send()
 
 
 def row_blocks(rows):
-    small = SUBL * SUBL
-    edges = [0, small] + list(range(2 * small, rows + 1, 2 * small))
+    edges = [0, LANES // 4, LANES // 2] + list(range(LANES, rows + 1, LANES))
     return [(low, high - low) for low, high in zip(edges, edges[1:])]
 
 

time: 15.5 us -> 16.2 us (1.045)
  Pallas kernels: 15.3 us -> 16 us
    pallas_call x1, Pallas kernels: 11.7 us -> 12.4 us  [body(): pl.pallas_call(functools.partial(spectra_kernel, (n_inp, n_frq, n_loc, fr...]
where the time goes in v8:
time: 16.2 us; the launch traced here: 16 us
  Pallas kernels  16 us (99%)
    pallas_call x1, Pallas kernels, body(): pl.pallas_call(functools.partial(spectra_kernel, (n_inp, n_frq, n_loc, fr...  12.4 us
    pallas_call x1, Pallas kernels, body(): pl.pallas_call(functools.partial(gram_kernel, (n_inp, n_frq, n_loc, n_q,...  3.65 us

profile of v8, /device:TPU:0, one launch (start us, length us, event | category | flops | bytes accessed | tf_op | source)
XLA Modules:
  0.0 16.0 jit_solution(11932473834711106103)
XLA Ops:
  0.0 12.4 %spectra_exchange.1.msg_hbm = f32[256,128]{1,0:T(8,128)} custom-call(bf16[64,16,4,128]{3,2,1,0:T(4,128)(2,1)} %bitcast.11, bf16[192,2048]{1,0:T(8,128)(2,1)} %bitcast.12, f32[32,2048]{1,0:T(8,128)} %constant.2.clone.table_hbm, f32[4,2048]{1,0:T(4,128)} %window_hbm.1), custom_call_target="tpu_custom_call" | custom-call | tf_op jit(solution)/shard_map/spectra_exchange/pallas_call | solution.py:298
  12.4 3.6 %gram.1 = f32[8192,128]{1,0:T(8,128)} custom-call(f32[256,128]{1,0:T(8,128)} %spectra_exchange.1.msg_hbm), custom_call_target="tpu_custom_call" | custom-call | tf_op jit(solution)/shard_map/gram/pallas_call | solution.py:326

commit v9 on v7

--- a/solution.py
+++ b/solution.py
@@ -33,18 +33,24 @@
     return out
 
 
+def ahead_of(index, steps, size):
+    moved = index + steps
+    return jnp.where(moved >= size, moved - size, moved)
+
+
 def to_others(n_inp, n_frq, my_inp, my_frq, act):
     def group(ahead, low):
-        to_inp = lax.rem(my_inp + ahead, n_inp)
+        to_inp = ahead_of(my_inp, ahead, n_inp)
         for turn in range(low, n_frq):
-            act(to_inp, lax.rem(my_frq + turn, n_frq))
+            act(to_inp, ahead_of(my_frq, turn, n_frq) if turn else my_frq)
 
     if n_inp * n_frq <= 32:
         for step in range(n_inp - 1):
             group((n_inp // 2 + step) % n_inp if step < n_inp // 2 else n_inp - 1 - step, 0)
     else:
         lax.fori_loop(1, n_inp, lambda step, carry: (group(step, 0), carry)[1], 0)
-    group(0, 1)
+    for turn in range(1, n_frq):
+        act(my_inp, ahead_of(my_frq, turn, n_frq))
 
 
 def spectra_kernel(

time: 15.5 us -> 15.5 us (level)
  no operation moved by 1% of the time
where the time goes in v9:
time: 15.5 us; the launch traced here: 15.3 us
  Pallas kernels  15.3 us (99%)
    pallas_call x1, Pallas kernels, body(): pl.pallas_call(functools.partial(spectra_kernel, (n_inp, n_frq, n_loc, fr...  11.7 us
    pallas_call x1, Pallas kernels, body(): pl.pallas_call(functools.partial(gram_kernel, (n_inp, n_frq, n_loc, n_q,...  3.64 us

profile of v9, /device:TPU:0, one launch (start us, length us, event | category | flops | bytes accessed | tf_op | source)
XLA Modules:
  0.0 15.3 jit_solution(14497326668014817560)
XLA Ops:
  0.0 11.7 %spectra_exchange.1.msg_hbm = f32[256,128]{1,0:T(8,128)} custom-call(bf16[64,16,4,128]{3,2,1,0:T(4,128)(2,1)} %bitcast.11, bf16[192,2048]{1,0:T(8,128)(2,1)} %bitcast.12, f32[32,2048]{1,0:T(8,128)} %constant.2.clone.table_hbm, f32[4,2048]{1,0:T(4,128)} %window_hbm.1), custom_call_target="tpu_custom_call" | custom-call | tf_op jit(solution)/shard_map/spectra_exchange/pallas_call | solution.py:316
  11.7 3.6 %gram.1 = f32[8192,128]{1,0:T(8,128)} custom-call(f32[256,128]{1,0:T(8,128)} %spectra_exchange.1.msg_hbm), custom_call_target="tpu_custom_call" | custom-call | tf_op jit(solution)/shard_map/gram/pallas_call | solution.py:344

commit v10 on v5

--- a/solution.py
+++ b/solution.py
@@ -253,34 +253,25 @@
     h, m, l = split_bf16(jnp.concatenate([left, swapped], axis=1), 3)
     left_scr[...] = jnp.concatenate([h, h, m, h, l, m] + spare, axis=0).T
     right_scr[...] = right
-    per_row = 2 * inputs // LANES
-    block = SUBL * SUBL
-    blocks = rows_dev // block
-
-    def out_copy(step):
-        rows = pl.ds(pl.multiple_of(step * block * per_row, block * per_row), block * per_row)
-        return pltpu.make_async_copy(vis_scr.at[rows], out_hbm.at[rows], out_sem.at[step])
-
-    def one_block(step, carry):
-        row = pl.multiple_of(step * block, block)
-        sides = [left_scr[pl.ds(part * rows_dev + row, block), :] for part in range(2)]
+    width = 2 * LANES
+    copies = []
+    for block in range(inputs // width):
         vis = jnp.dot(
-            jnp.concatenate(sides, axis=0), right_scr[...], preferred_element_type=jnp.float32
+            left_scr[...],
+            right_scr[:, block * width : (block + 1) * width],
+            preferred_element_type=jnp.float32,
         )
-        for part in range(2):
-            for r in range(0, block, SUBL):
-                for tile in range(inputs // LANES):
-                    at = (row + r) * per_row + 2 * tile + part
-                    vis_scr[pl.ds(at, SUBL, stride=per_row), :] = vis[
-                        part * block + r : part * block + r + SUBL,
-                        tile * LANES : (tile + 1) * LANES,
-                    ]
-        out_copy(step).start()
-        return carry
-
-    lax.fori_loop(0, blocks, one_block, 0)
-    for step in range(blocks):
-        out_copy(step).wait()
+        for tile in range(2):
+            for part in range(2):
+                at = 2 * (2 * block + tile) + part
+                vis_scr[at] = vis[
+                    part * rows_dev : (part + 1) * rows_dev, tile * LANES : (tile + 1) * LANES
+                ]
+                copy = pltpu.make_async_copy(vis_scr.at[at], out_hbm.at[:, at], out_sem.at[at])
+                copy.start()
+                copies.append(copy)
+    for copy in copies:
+        copy.wait()
 
 
 def body(n_inp, n_frq, voltages, history, window):
@@ -331,7 +322,7 @@
             gram_kernel,
             (n_inp, n_frq, n_loc, n_q, msg_rows, frames * n_frq, rows_dev),
         ),
-        out_shape=jax.ShapeDtypeStruct((rows_dev * per_row, LANES), jnp.float32),
+        out_shape=jax.ShapeDtypeStruct((rows_dev, per_row, LANES), jnp.float32),
         in_specs=[pl.BlockSpec(memory_space=pl.ANY)],
         out_specs=pl.BlockSpec(memory_space=pl.ANY),
         scratch_shapes=[
@@ -339,9 +330,9 @@
             pltpu.VMEM((depth, inputs), jnp.float32),
             pltpu.VMEM((2 * rows_dev, stack), jnp.bfloat16),
             pltpu.VMEM((stack, inputs), jnp.bfloat16),
-            pltpu.VMEM((rows_dev * per_row, LANES), jnp.float32),
+            pltpu.VMEM((per_row, rows_dev, LANES), jnp.float32),
             pltpu.SemaphoreType.DMA,
-            pltpu.SemaphoreType.DMA((rows_dev // (SUBL * SUBL),)),
+            pltpu.SemaphoreType.DMA((per_row,)),
         ],
         compiler_params=pltpu.CompilerParams(vmem_limit_bytes=60 * 2**20),
         name="gram",

time: 16 us -> 15.2 us (0.950)
  Pallas kernels: 15.8 us -> 15.1 us
    pallas_call x1, Pallas kernels: 4.28 us -> 3.53 us  [body(): pl.pallas_call(functools.partial(gram_kernel, (n_inp, n_frq, n_loc, n_q,...]
where the time goes in v10:
time: 15.2 us; the launch traced here: 15.1 us
  Pallas kernels  15.1 us (99%)
    pallas_call x1, Pallas kernels, body(): pl.pallas_call(functools.partial(spectra_kernel, (n_inp, n_frq, n_loc, fr...  11.5 us
    pallas_call x1, Pallas kernels, body(): pl.pallas_call(functools.partial(gram_kernel, (n_inp, n_frq, n_loc, n_q,...  3.53 us

profile of v10, /device:TPU:0, one launch (start us, length us, event | category | flops | bytes accessed | tf_op | source)
XLA Modules:
  0.0 15.1 jit_solution(5034089278611745837)
XLA Ops:
  0.0 11.5 %spectra_exchange.1.msg_hbm = f32[256,128]{1,0:T(8,128)} custom-call(bf16[64,4,2048]{2,1,0:T(4,128)(2,1)} %x_hbm.1, bf16[192,2048]{1,0:T(8,128)(2,1)} %bitcast.8, f32[32,2048]{1,0:T(8,128)} %constant.2.clone.table_hbm, f32[4,2048]{1,0:T(4,128)} %window_hbm.1), custom_call_target="tpu_custom_call" | custom-call | tf_op jit(solution)/shard_map/spectra_exchange/pallas_call | solution.py:292
  11.6 3.5 %gram.1 = f32[512,16,128]{2,1,0:T(8,128)} custom-call(f32[256,128]{1,0:T(8,128)} %spectra_exchange.1.msg_hbm), custom_call_target="tpu_custom_call" | custom-call | tf_op jit(solution)/shard_map/gram/pallas_call | solution.py:320
